TPU v7x, 512 devices: a whole 4x8x8 slice. The times are simulated.
512 devices in a mesh: rep: 8 (over z), ep: 64 (over x, y, core).
Axes of the slice: x: 4, y: 8, z: 8, core: 2. Of those that a mesh axis runs over, the one named last changes fastest.
Arguments:
- queries: bfloat16 [2048, 2, 64, 576], P(('rep', 'ep')), may hold values from -8 to 8
- latent_key_cache: bfloat16 [2048, 256, 576], P(('rep', 'ep')), may hold values from -5 to 5
- fresh_latent_keys: bfloat16 [2048, 2, 576], P(('rep', 'ep')), may hold values from -5 to 5
- lengths: int32 [2048], P(('rep', 'ep')), may hold values from 64 to 256
- accepted: int32 [2048], P(('rep', 'ep')), may hold values 0 or 1
- hidden: bfloat16 [2048, 2, 3584], P(('rep', 'ep')), may hold values from -6 to 6
- norm_gain: float32 [3584], replicated, may hold values from 0.5 to 1.5
- expert_ids: int32 [2048, 2, 8], P(('rep', 'ep')), may hold values from 0 to 63, all different within a row; in each aligned block of 8 rows (0 to 7, 8 to 15, ..., all dimensions but the last counted through in order) at most 2 rows name the same one
- router_weights: bfloat16 [2048, 2, 8], P(('rep', 'ep')), may hold values from 0.099609375 to 0.59765625
- gate_weight: bfloat16 [64, 3584, 1024], P('ep', None, 'rep'), may hold values from -0.09375 to 0.09375
- up_weight: bfloat16 [64, 3584, 1024], P('ep', None, 'rep'), may hold values from -0.09375 to 0.09375
- down_weight: bfloat16 [64, 1024, 3584], P('ep', None, 'rep'), may hold values from -0.1875 to 0.1875
Outputs:
- attended: bfloat16 [2048, 2, 64, 512], P(('rep', 'ep'))
- routed: bfloat16 [2048, 2, 3584], P(('rep', 'ep'))
Inputs may be any that keep to these rules, and one draw needn't show every extreme that they name: `expert_ids`: within the rows of one device (aligned blocks of 8 rows) no expert is named by more than 2 rows, and each row names different experts.
All inputs are finite; a program needn't handle non-finite values. No bound on the sum of `accepted` on one device may be relied on, other than what follows from the above.
Results may differ from a plain program's by a relative error of at most 0.0071.
Values may be sent and summed in bfloat16 or wider, within the bound.
No kernel may reach another device: no remote copies, remote signals or barrier semaphores. Data moves between devices by JAX's collectives and lax.ppermute only.
A program may use at most 64 MiB of HBM per device.

v0:
```python
from functools import partial

import jax
import jax.numpy as jnp
from jax import lax
from jax.sharding import PartitionSpec as P

LATENT_WIDTH = 512


score_scale = 192.0 ** (-0.5)


def fill_slots(rows_in, dest, slots):
    count = rows_in.shape[0]
    picks = dest.shape[1]
    target = jnp.where(dest >= 0, dest, slots).reshape(-1)
    owner = (
        jnp.full((slots,), count, jnp.int32)
        .at[target]
        .set(jnp.repeat(jnp.arange(count, dtype=jnp.int32), picks), mode="drop")
    )
    padded = jnp.concatenate([rows_in, jnp.zeros((1, rows_in.shape[1]), rows_in.dtype)], 0)
    return padded[owner]


def per_device(
    queries,
    latent_key_cache,
    fresh_latent_keys,
    lengths,
    accepted,
    hidden,
    norm_gain,
    expert_ids,
    router_weights,
    gate_weight,
    up_weight,
    down_weight,
):
    nreq = queries.shape[0]
    cache_len = latent_key_cache.shape[1]
    feature_width = hidden.shape[2]
    picks = expert_ids.shape[2]
    nrep = lax.axis_size("rep")
    experts = lax.axis_size("ep")
    slice_width = feature_width // nrep
    s_old = (
        jnp.einsum("rthc,rkc->rthk", queries, latent_key_cache, preferred_element_type=jnp.float32)
        * score_scale
    )
    s_new = (
        jnp.einsum("rthc,rnc->rthn", queries, fresh_latent_keys, preferred_element_type=jnp.float32)
        * score_scale
    )
    valid_old = jnp.arange(cache_len, dtype=jnp.int32)[None, :] < lengths[:, None]
    valid_new = jnp.arange(2, dtype=jnp.int32)[None, :] <= jnp.arange(2, dtype=jnp.int32)[:, None]
    s_old = jnp.where(valid_old[:, None, None, :], s_old, -jnp.inf)
    s_new = jnp.where(valid_new[None, :, None, :], s_new, -jnp.inf)
    top = jnp.maximum(jnp.max(s_old, -1, keepdims=True), jnp.max(s_new, -1, keepdims=True))
    e_old = jnp.exp(s_old - top)
    e_new = jnp.exp(s_new - top)
    total = jnp.sum(e_old, -1, keepdims=True) + jnp.sum(e_new, -1, keepdims=True)
    cached_probability = (e_old / total).astype(jnp.bfloat16)
    fresh_probability = (e_new / total).astype(jnp.bfloat16)
    out = jnp.einsum(
        "zlim,zmd->zlid",
        cached_probability,
        latent_key_cache[:, :, :LATENT_WIDTH],
        preferred_element_type=jnp.float32,
    )
    out = out + jnp.einsum(
        "swbd,sdo->swbo",
        fresh_probability,
        fresh_latent_keys[:, :, :LATENT_WIDTH],
        preferred_element_type=jnp.float32,
    )
    row_live = jnp.stack([jnp.ones_like(accepted), accepted], 1)
    attended = (out * row_live.astype(jnp.float32)[:, :, None, None]).astype(jnp.bfloat16)
    rows = nreq * 2
    capacity = max(2, (rows * picks + experts - 1) // experts)
    x = hidden.reshape(rows, feature_width).astype(jnp.float32)
    meansq = jnp.mean(x * x, -1, keepdims=True)
    normed = (x * lax.rsqrt(meansq + 1e-06) * norm_gain).astype(jnp.bfloat16)
    pair_live = jnp.repeat(row_live.reshape(rows), picks)
    ids = expert_ids.reshape(rows * picks)
    onehot = (ids[:, None] == jnp.arange(experts, dtype=jnp.int32)[None, :]).astype(
        jnp.int32
    ) * pair_live[:, None]
    before = jnp.cumsum(onehot, 0) - onehot
    slot = jnp.sum(before * onehot, 1)
    dest = jnp.where(pair_live > 0, ids * capacity + slot, -1).reshape(rows, picks)
    weights = router_weights.reshape(rows, picks)
    slots = experts * capacity
    col_x, col_dest = (
        lax.all_gather(normed, "rep", axis=0, tiled=True),
        lax.all_gather(dest, "rep", axis=0, tiled=True),
    )
    col_dest = col_dest.reshape(nrep, rows, picks)
    buffer = jax.vmap(partial(fill_slots, slots=slots))(
        col_x.reshape(nrep, rows, feature_width), col_dest
    )
    buffer = buffer.reshape(nrep, experts, capacity, feature_width)
    expert_in = lax.all_to_all(buffer, "ep", split_axis=1, concat_axis=1, tiled=True)
    flat = expert_in.reshape(-1, feature_width)
    gate = jnp.dot(flat, gate_weight[0], preferred_element_type=jnp.float32)
    up = jnp.dot(flat, up_weight[0], preferred_element_type=jnp.float32)
    inner = (jax.nn.silu(gate) * up).astype(jnp.bfloat16)
    down_local = down_weight[0]
    expert_out = jnp.dot(
        lax.all_gather(inner, "rep", axis=1, tiled=True),
        down_local,
        preferred_element_type=jnp.float32,
    ).astype(jnp.bfloat16)
    expert_out = expert_out.reshape(nrep, experts, capacity, slice_width)
    back = lax.all_to_all(
        lax.all_to_all(expert_out, "rep", split_axis=0, concat_axis=0, tiled=True),
        "ep",
        split_axis=1,
        concat_axis=1,
        tiled=True,
    )
    chosen = back.reshape(nrep, slots, slice_width)[:, jnp.maximum(dest, 0)]
    scaled = jnp.where(dest >= 0, weights.astype(jnp.float32), 0.0)
    mixed = jnp.einsum("srkd,rk->rsd", chosen.astype(jnp.float32), scaled).reshape(
        rows, feature_width
    )
    routed = mixed.reshape(nreq, 2, feature_width).astype(jnp.bfloat16)
    return (attended, routed)


def solution(mesh):
    in_specs = (
        P(("rep", "ep"), None, None, None),
        P(("rep", "ep"), None, None),
        P(("rep", "ep"), None, None),
        P(("rep", "ep")),
        P(("rep", "ep")),
        P(("rep", "ep"), None, None),
        P(),
        P(("rep", "ep"), None, None),
        P(("rep", "ep"), None, None),
        P("ep", None, "rep"),
        P("ep", None, "rep"),
        P("ep", None, "rep"),
    )
    out_specs = (P(("rep", "ep"), None, None, None), P(("rep", "ep"), None, None))
    return jax.shard_map(
        per_device, mesh=mesh, in_specs=in_specs, out_specs=out_specs, check_vma=False
    )
```

profile of v0, /device:TPU:1, one launch (start us, length us, event | category | flops | bytes accessed | tf_op | source)
XLA Modules:
  0.0 482.2 jit_solution(2903654991053115515)
XLA Ops:
  7.2 0.8 eq.15
  8.1 0.7 broadcast_multiply_fusion
  8.8 0.8 reshape.191
  9.6 1.0 multiply_reduce_fusion
  10.6 0.7 copy.51
  12.1 0.8 convert_select_fusion
  12.9 25.3 %all_gather.10 = s32[64,8]{1,0:T(8,128)S(1)} all-gather(s32[8,8]{1,0:T(8,128)S(1)} %get-tuple-element.3), channel_id=1, replica_groups=mesh['rep'=8,'ep'=64] {'rep'}, dimensions={0}, use_global_device_ids=true | all-gather | bytes 2304 | tf_op jit(solution)/shard_map/all_gather | solution.py:97
  38.5 22.1 %scatter_fusion = s32[8,128]{1,0:T(8,128)S(1)} fusion(s32[8,128]{1,0:T(8,128)S(1)} %broadcast_in_dim.78, s32[512]{0:T(512)S(1)} %reshape.207, s32[512]{0:T(512)S(1)} %reshape.209), kind=kCustom, calls=%fused_computation.2 | custom fusion | bytes 10240 | tf_op jit(solution)/shard_map/vmap()/scatter | solution.py:21
  60.8 19.1 %all_gather.9 = bf16[64,3584]{1,0:T(8,128)(2,1)S(1)} all-gather(bf16[8,3584]{1,0:T(8,128)(2,1)S(1)} %multiply_convert_fusion), channel_id=1, replica_groups=mesh['rep'=8,'ep'=64] {'rep'}, dimensions={0}, use_global_device_ids=true | all-gather | bytes 516096 | tf_op jit(solution)/shard_map/all_gather | solution.py:96
  80.1 32.1 %gather_fusion.1 = bf16[1024,3584]{1,0:T(8,128)(2,1)} fusion(bf16[8,9,3584]{2,0,1:T(8,128)(2,1)S(1)} %concatenate.3, s32[1024]{0:T(1024)S(1)} %fusion.31), kind=kCustom, calls=%fused_computation.1 | custom fusion | bytes 14688256 | tf_op jit(solution)/shard_map/vmap()/gather | solution.py:24
  112.2 14.9 %reshape.187 = bf16[8,64,2,3584]{3,2,1,0:T(2,128)(2,1)} reshape(bf16[1024,3584]{1,0:T(8,128)(2,1)} %gather_fusion.1) | data formatting | bytes 14680064 | tf_op jit(solution)/shard_map/reshape | solution.py:103
  127.1 9.1 %copy.35 = bf16[8,64,2,3584]{3,2,0,1:T(2,128)(2,1)S(1)} copy(bf16[8,64,2,3584]{3,2,1,0:T(2,128)(2,1)} %reshape.187) | data formatting | bytes 14680064 | tf_op jit(solution)/shard_map/reshape | solution.py:103
  136.2 186.6 %all_to_all.15 = bf16[8,64,2,3584]{3,2,0,1:T(2,128)(2,1)S(1)} all-to-all(bf16[8,64,2,3584]{3,2,0,1:T(2,128)(2,1)S(1)} %copy.35), channel_id=1, replica_groups=mesh['rep'=8,'ep'=64] {'ep'}, dimensions={1} | all-to-all | bytes 14680064 | tf_op jit(solution)/shard_map/all_to_all | solution.py:104
  322.8 6.2 %copy.36 = bf16[8,64,2,3584]{3,2,1,0:T(2,128)(2,1)} copy(bf16[8,64,2,3584]{3,2,0,1:T(2,128)(2,1)S(1)} %all_to_all.15) | data formatting | bytes 14680064 | tf_op jit(solution)/shard_map/all_to_all | solution.py:104
  329.0 15.5 %reshape.188 = bf16[1024,3584]{1,0:T(8,128)(2,1)} reshape(bf16[8,64,2,3584]{3,2,1,0:T(2,128)(2,1)} %copy.36) | data formatting | bytes 14680064 | tf_op jit(solution)/shard_map/reshape | solution.py:105
  344.5 5.3 %fusion.11 = f32[1024,128]{1,0:T(8,128)S(1)} fusion(bf16[1024,3584]{1,0:T(8,128)(2,1)} %reshape.188, bf16[1,3584,128]{2,1,0:T(8,128)(2,1)S(1)} %copy-done.6), kind=kOutput, calls=%fused_computation.19 | convolution fusion | flops 939524096 | bytes 8781824 | tf_op jit(solution)/shard_map/dot_general | solution.py:106
  349.9 2.8 fusion.3
  352.7 40.6 %all-gather.2.cloned.1.call-done = bf16[1024,1024]{1,0:T(8,128)(2,1)} async-done(((bf16[1024,128]{1,0:T(8,128)(2,1)}), bf16[1024,1024]{1,0:T(8,128)(2,1)}) %all-gather.2.cloned.1.call-update) | async-done | bytes 2097168 | tf_op jit(solution)/shard_map/all_gather | solution.py:111
  393.3 3.7 convolution_convert_fusion
  397.0 1.6 copy.37
  398.5 1.3 reshape.189
  399.8 3.6 all-to-all-start.1
  403.5 24.9 %all-to-all-done.1 = bf16[8,64,2,448]{3,2,1,0:T(2,128)(2,1)S(1)} async-done(((bf16[8,64,2,448]{3,2,1,0:T(2,128)(2,1)}), bf16[8,64,2,448]{3,2,1,0:T(2,128)(2,1)S(1)}, u32[]{:S(2)}, u32[]{:S(2)}) %all-to-all-start.1) | async-done | bytes 917536 | tf_op jit(solution)/shard_map/all_to_all | solution.py:117
  428.4 2.2 copy.38
  430.6 14.3 %all-to-all-start.2 = ((bf16[8,64,2,448]{3,2,0,1:T(2,128)(2,1)}), bf16[8,64,2,448]{3,2,0,1:T(2,128)(2,1)S(1)}, u32[]{:S(2)}, u32[]{:S(2)}) async-start(bf16[8,64,2,448]{3,2,0,1:T(2,128)(2,1)} %copy.38), calls=%async_computation.2 | async-start | bytes 2097152 | tf_op jit(solution)/shard_map/all_to_all | solution.py:116
  445.2 1.5 fusion.36
  446.7 1.6 fusion.35
  448.6 0.5 fusion.6
  449.1 1.2 fusion.1
  450.3 23.2 %all-to-all-done.2 = bf16[8,64,2,448]{3,2,0,1:T(2,128)(2,1)S(1)} async-done(((bf16[8,64,2,448]{3,2,0,1:T(2,128)(2,1)}), bf16[8,64,2,448]{3,2,0,1:T(2,128)(2,1)S(1)}, u32[]{:S(2)}, u32[]{:S(2)}) %all-to-all-start.2) | async-done | bytes 917536 | tf_op jit(solution)/shard_map/all_to_all | solution.py:116
  473.7 0.6 gather_fusion
  474.6 0.8 convert_element_type.57
  (58 shorter events, 2.9 us)
Async XLA Ops:
  7.2 386.1 %copy-start = (bf16[1,1024,448]{1,2,0:T(8,128)(2,1)S(1)}, bf16[1,1024,448]{1,2,0:T(8,128)(2,1)}, u32[]{:S(2)}) copy-start(bf16[1,1024,448]{1,2,0:T(8,128)(2,1)} %param.23) | copy-start | bytes 2752516
  7.2 53.5 %copy-start.3 = (f32[3584]{0:T(1024)S(1)}, f32[3584]{0:T(1024)}, u32[]{:S(2)}) copy-start(f32[3584]{0:T(1024)} %param.18) | copy-start | bytes 43012
  7.2 386.1 %all-gather.2.cloned.1.call-start = ((), (), s32[]{:S(2)}) async-start(), calls=%async_computation.3 | async-start | bytes 2359296 | tf_op jit(solution)/shard_map/all_gather | solution.py:111
  329.0 15.5 %copy-start.6 = (bf16[1,3584,128]{2,1,0:T(8,128)(2,1)S(1)}, bf16[1,3584,128]{2,1,0:T(8,128)(2,1)}, u32[]{:S(2)}) copy-start(bf16[1,3584,128]{2,1,0:T(8,128)(2,1)} %param.21) | copy-start | bytes 2752516
  344.5 5.3 %copy-start.1 = (bf16[1024,3584]{1,0:T(8,128)(2,1)S(1)}, bf16[1024,3584]{1,0:T(8,128)(2,1)}, u32[]{:S(2)}) copy-start(bf16[1024,3584]{1,0:T(8,128)(2,1)} %reshape.188) | copy-start | bytes 22020100
  344.5 5.4 %copy-start.7 = (bf16[1,3584,128]{2,1,0:T(8,128)(2,1)S(1)}, bf16[1,3584,128]{2,1,0:T(8,128)(2,1)}, u32[]{:S(2)}) copy-start(bf16[1,3584,128]{2,1,0:T(8,128)(2,1)} %param.22) | copy-start | bytes 2752516
  396.9 47.9 %copy-start.5 = (s32[4]{0:T(128)S(1)}, s32[4]{0:T(128)}, u32[]{:S(2)}) copy-start(s32[4]{0:T(128)} %param.16) | copy-start | bytes 52
  396.9 48.1 %copy-start.8 = (s32[4]{0:T(128)S(1)}, s32[4]{0:T(128)}, u32[]{:S(2)}) copy-start(s32[4]{0:T(128)} %param.15) | copy-start | bytes 52
  396.9 48.2 %copy-start.4 = (bf16[4,2,576]{2,1,0:T(2,128)(2,1)S(1)}, bf16[4,2,576]{2,1,0:T(2,128)(2,1)}, u32[]{:S(2)}) copy-start(bf16[4,2,576]{2,1,0:T(2,128)(2,1)} %param.14) | copy-start | bytes 27652
  397.0 49.7 %copy-start.2 = (bf16[4,256,576]{1,2,0:T(8,128)(2,1)S(1)}, bf16[4,256,576]{1,2,0:T(8,128)(2,1)}, u32[]{:S(2)}) copy-start(bf16[4,256,576]{1,2,0:T(8,128)(2,1)} %param.13) | copy-start | bytes 3538948
  399.8 28.6 %all-to-all-start.1 = ((bf16[8,64,2,448]{3,2,1,0:T(2,128)(2,1)}), bf16[8,64,2,448]{3,2,1,0:T(2,128)(2,1)S(1)}, u32[]{:S(2)}, u32[]{:S(2)}) async-start(bf16[8,64,2,448]{3,2,1,0:T(2,128)(2,1)} %reshape.189), calls=%async_computation.1 | async-start | bytes 2097152 | tf_op jit(solution)/shard_map/all_to_all | solution.py:117
  430.6 42.9 %all-to-all-start.2 = ((bf16[8,64,2,448]{3,2,0,1:T(2,128)(2,1)}), bf16[8,64,2,448]{3,2,0,1:T(2,128)(2,1)S(1)}, u32[]{:S(2)}, u32[]{:S(2)}) async-start(bf16[8,64,2,448]{3,2,0,1:T(2,128)(2,1)} %copy.38), calls=%async_computation.2 | async-start | bytes 2097152 | tf_op jit(solution)/shard_map/all_to_all | solution.py:116
Sparse Core Ops, SparseCore 0:
  352.8 40.4 all-gather.1
where the time goes:
time: 483 us; the launch traced here: 482 us
  blocking collectives  231 us (48%)
  local copies, waits for them, and re-layouts  110 us (23%)
  waiting for transfers between devices  88.7 us (18%)
  starting transfers between devices  17.9 us (4%)
  matrix products  16.7 us (3%)
  between operations  14.3 us (3%)
    all_to_all x1, blocking collectives, per_device(): lax.all_to_all(buffer, 'ep', split_axis=1, concat_axis=1, tiled=True)  187 us
    all_gather x1, waiting for transfers between devices, per_device(): lax.all_gather(inner, 'rep', axis=1, tiled=True)  40.6 us
    gather x1, local copies, waits for them, and re-layouts, fill_slots(): return padded[owner]  32.1 us
    all_gather x1, blocking collectives, per_device(): lax.all_gather(dest, 'rep', axis=0, tiled=True)  25.3 us
    all_to_all x1, waiting for transfers between devices, per_device(): lax.all_to_all(expert_out, 'rep', split_axis=0, concat_axis=0, tiled=True)  24.9 us
    reshape x2, local copies, waits for them, and re-layouts, per_device(): buffer = buffer.reshape(nrep, experts, capacity, feature_width)  24 us
    all_to_all x1, waiting for transfers between devices, per_device(): lax.all_to_all(lax.all_to_all(expert_out, 'rep', split_axis=0, concat_axi...  23.2 us
    scatter x2, local copies, waits for them, and re-layouts, fill_slots(): owner = jnp.full((slots,), count, jnp.int32).at[target].set(jnp.repeat(jn...  22.2 us
  transfers between devices with their start and end apart: 3, of which 3 were waited for; matrix products, arithmetic and copies ran while one was open for 1% of the time, Pallas kernels for 0%

commit v1 on v0

v1 whole, which is shorter than its diff:
```python
from functools import partial

import jax
import jax.numpy as jnp
from jax import lax
from jax.experimental import pallas as pl
from jax.experimental.pallas import tpu as pltpu
from jax.sharding import PartitionSpec as P

LATENT_WIDTH = 512

score_scale = 192.0 ** (-0.5)
SMEM = pl.BlockSpec(memory_space=pltpu.SMEM)
VMEM = pl.BlockSpec(memory_space=pltpu.VMEM)
limit = pltpu.CompilerParams(vmem_limit_bytes=48 * 1024 * 1024)


def prepare_kernel(hidden_ref, gain_ref, ids_ref, weights_ref, live_ref, rows_ref, mix_ref):
    rows, width = hidden_ref.shape
    x = hidden_ref[...].astype(jnp.float32)
    meansq = jnp.mean(x * x, -1, keepdims=True)
    normed = x * lax.rsqrt(meansq + 1e-06) * gain_ref[...]
    rows_ref[:, :width] = normed.astype(jnp.bfloat16)

    slots = mix_ref.shape[1]
    lane = lax.broadcasted_iota(jnp.int32, (rows, slots), 1)
    live = live_ref[...].astype(jnp.float32)
    named = jnp.zeros((rows, slots), jnp.float32)
    weight = jnp.zeros((rows, slots), jnp.float32)
    for p in range(ids_ref.shape[1]):
        hit = lane // 2 == ids_ref[:, p : p + 1]
        named += jnp.where(hit, live, 0.0)
        weight += jnp.where(hit, weights_ref[:, p : p + 1].astype(jnp.float32), 0.0)
    row = lax.broadcasted_iota(jnp.int32, (rows, slots), 0)
    rank = jnp.zeros((rows, slots), jnp.float32)
    for r in range(rows - 1):
        rank += jnp.where(row > r, named[r : r + 1, :], 0.0)
    taken = jnp.where(rank == (lane % 2).astype(jnp.float32), named, 0.0)
    rows_ref[:, width:] = taken.astype(jnp.bfloat16)
    mix_ref[...] = (taken * weight).astype(jnp.bfloat16)


def dispatch_kernel(rows_ref, out_ref):
    slots, width = out_ref.shape
    taken = rows_ref[:, width:]
    step = 512
    for c in range(0, width, step):
        out_ref[:, c : c + step] = lax.dot_general(
            taken,
            rows_ref[:, c : c + step],
            (((0,), (0,)), ((), ())),
            preferred_element_type=jnp.float32,
        ).astype(jnp.bfloat16)


def inner_piece(rows, weight):
    units = weight.shape[1] // 2
    both = jnp.dot(rows, weight, preferred_element_type=jnp.float32)
    g, u = both[:, :units], both[:, units:]
    return (g / (1.0 + jnp.exp(-g)) * u).astype(jnp.bfloat16)


def inner_kernel(weight_ref, *refs):
    out_ref = refs[-1]
    for i, rows_ref in enumerate(refs[:-1]):
        out_ref[i] = inner_piece(rows_ref[...], weight_ref[...])


def last_inner_kernel(places, me_ref, weight_ref, *refs):
    out_ref = refs[-1]
    count = out_ref.shape[0]
    new, old = refs[:2], refs[2:-1]
    for place, rows_ref in zip(places[:2], new):
        out_ref[lax.rem(me_ref[0] + place + count, count)] = inner_piece(
            rows_ref[...], weight_ref[...]
        )
    for i, place in enumerate(places[2:]):
        out_ref[lax.rem(me_ref[0] + place + count, count)] = old[i // 2][i % 2]


def down_kernel(inner_ref, weight_ref, out_ref):
    full = jnp.concatenate([inner_ref[r] for r in range(inner_ref.shape[0])], axis=1)
    out_ref[...] = lax.dot_general(
        full, weight_ref[...], (((1,), (1,)), ((), ())), preferred_element_type=jnp.float32
    ).astype(jnp.bfloat16)


def mix_kernel(mix_ref, back_ref, out_ref):
    out_ref[...] = jnp.dot(
        mix_ref[...], back_ref[...], preferred_element_type=jnp.float32
    ).astype(jnp.bfloat16)


def attend(queries, latent_key_cache, fresh_latent_keys, lengths, row_live):
    cache_len = latent_key_cache.shape[1]
    s_old = (
        jnp.einsum("rthc,rkc->rthk", queries, latent_key_cache, preferred_element_type=jnp.float32)
        * score_scale
    )
    s_new = (
        jnp.einsum("rthc,rnc->rthn", queries, fresh_latent_keys, preferred_element_type=jnp.float32)
        * score_scale
    )
    valid_old = jnp.arange(cache_len, dtype=jnp.int32)[None, :] < lengths[:, None]
    valid_new = jnp.arange(2, dtype=jnp.int32)[None, :] <= jnp.arange(2, dtype=jnp.int32)[:, None]
    s_old = jnp.where(valid_old[:, None, None, :], s_old, -jnp.inf)
    s_new = jnp.where(valid_new[None, :, None, :], s_new, -jnp.inf)
    top = jnp.maximum(jnp.max(s_old, -1, keepdims=True), jnp.max(s_new, -1, keepdims=True))
    e_old = jnp.exp(s_old - top)
    e_new = jnp.exp(s_new - top)
    total = jnp.sum(e_old, -1, keepdims=True) + jnp.sum(e_new, -1, keepdims=True)
    cached_probability = (e_old / total).astype(jnp.bfloat16)
    fresh_probability = (e_new / total).astype(jnp.bfloat16)
    out = jnp.einsum(
        "zlim,zmd->zlid",
        cached_probability,
        latent_key_cache[:, :, :LATENT_WIDTH],
        preferred_element_type=jnp.float32,
    )
    out = out + jnp.einsum(
        "swbd,sdo->swbo",
        fresh_probability,
        fresh_latent_keys[:, :, :LATENT_WIDTH],
        preferred_element_type=jnp.float32,
    )
    return (out * row_live.astype(jnp.float32)[:, :, None, None]).astype(jnp.bfloat16)


def per_device(
    queries,
    latent_key_cache,
    fresh_latent_keys,
    lengths,
    accepted,
    hidden,
    norm_gain,
    expert_ids,
    router_weights,
    gate_weight,
    up_weight,
    down_weight,
):
    nreq = queries.shape[0]
    width = hidden.shape[2]
    picks = expert_ids.shape[2]
    nrep = lax.axis_size("rep")
    experts = lax.axis_size("ep")
    rows = nreq * 2
    units = gate_weight.shape[2]
    slots = 2 * experts
    row_live = jnp.stack([jnp.ones_like(accepted), accepted], 1)
    attended = attend(queries, latent_key_cache, fresh_latent_keys, lengths, row_live)

    all_down = lax.all_gather(
        jnp.swapaxes(down_weight[0], 0, 1), "rep", axis=0, tiled=True
    )
    tagged, mix = pl.pallas_call(
        prepare_kernel,
        out_shape=(
            jax.ShapeDtypeStruct((rows, width + slots), jnp.bfloat16),
            jax.ShapeDtypeStruct((rows, slots), jnp.bfloat16),
        ),
        in_specs=[VMEM] * 5,
        out_specs=(VMEM, VMEM),
        compiler_params=limit,
        name="prepare",
    )(
        hidden.reshape(rows, width),
        norm_gain.reshape(1, width),
        expert_ids.reshape(rows, picks),
        router_weights.reshape(rows, picks),
        row_live.reshape(rows, 1),
    )

    def to_experts(rows_in):
        buffer = pl.pallas_call(
            dispatch_kernel,
            out_shape=jax.ShapeDtypeStruct((slots, width), jnp.bfloat16),
            in_specs=[VMEM],
            out_specs=VMEM,
            compiler_params=limit,
            name="dispatch",
        )(rows_in)
        moved = lax.all_to_all(
            buffer.reshape(experts, 2, width), "ep", split_axis=0, concat_axis=0, tiled=True
        )
        return moved.reshape(slots, width)

    def shift(x, by):
        return lax.ppermute(x, "rep", [(i, (i + by) % nrep) for i in range(nrep)])

    both_weight = jnp.concatenate([gate_weight[0], up_weight[0]], axis=1)

    def inner_blocks(*blocks):
        n = len(blocks)
        return pl.pallas_call(
            inner_kernel,
            out_shape=jax.ShapeDtypeStruct((n, slots, units), jnp.bfloat16),
            in_specs=[VMEM] * (n + 1),
            out_specs=VMEM,
            compiler_params=limit,
            cost_estimate=pl.CostEstimate(
                flops=4 * n * slots * width * units,
                bytes_accessed=2 * width * (2 * units + n * slots),
                transcendentals=n * slots * units,
            ),
            name="inner",
        )(both_weight, *blocks)

    own = to_experts(tagged)
    far = to_experts(shift(tagged, nrep // 2))
    places, done = [], []
    up_block = down_block = own
    for s in range(1, nrep // 2):
        up_block, down_block = shift(up_block, 1), shift(down_block, -1)
        places = places + [-s, s]
        if s < nrep // 2 - 1:
            done.append(inner_blocks(up_block, down_block))
    places = places[-2:] + places[:-2] + [0, nrep // 2]
    done.append(inner_blocks(own, far))
    by_home = pl.pallas_call(
        partial(last_inner_kernel, places),
        out_shape=jax.ShapeDtypeStruct((nrep, slots, units), jnp.bfloat16),
        in_specs=[SMEM] + [VMEM] * (3 + len(done)),
        out_specs=VMEM,
        compiler_params=limit,
        name="last_inner",
    )(
        lax.axis_index("rep").astype(jnp.int32).reshape(1),
        both_weight,
        up_block,
        down_block,
        *done,
    )
    inner = lax.all_to_all(by_home, "rep", split_axis=0, concat_axis=0, tiled=True)
    columns = 512
    expert_out = pl.pallas_call(
        down_kernel,
        out_shape=jax.ShapeDtypeStruct((slots, width), jnp.bfloat16),
        grid=(width // columns,),
        in_specs=[
            pl.BlockSpec((nrep, slots, units), lambda i: (0, 0, 0)),
            pl.BlockSpec((columns, nrep * units), lambda i: (i, 0)),
        ],
        out_specs=pl.BlockSpec((slots, columns), lambda i: (0, i)),
        compiler_params=limit,
        name="down",
    )(inner, all_down)
    back = lax.all_to_all(
        expert_out.reshape(experts, 2, width), "ep", split_axis=0, concat_axis=0, tiled=True
    ).reshape(slots, width)
    routed = pl.pallas_call(
        mix_kernel,
        out_shape=jax.ShapeDtypeStruct((rows, width), jnp.bfloat16),
        in_specs=[VMEM] * 2,
        out_specs=VMEM,
        compiler_params=limit,
        name="mix",
    )(mix, back)
    return attended, routed.reshape(nreq, 2, width)


def solution(mesh):
    in_specs = (
        P(("rep", "ep"), None, None, None),
        P(("rep", "ep"), None, None),
        P(("rep", "ep"), None, None),
        P(("rep", "ep")),
        P(("rep", "ep")),
        P(("rep", "ep"), None, None),
        P(),
        P(("rep", "ep"), None, None),
        P(("rep", "ep"), None, None),
        P("ep", None, "rep"),
        P("ep", None, "rep"),
        P("ep", None, "rep"),
    )
    out_specs = (P(("rep", "ep"), None, None, None), P(("rep", "ep"), None, None))
    return jax.shard_map(
        per_device, mesh=mesh, in_specs=in_specs, out_specs=out_specs, check_vma=False
    )
```

time: 483 us -> 243 us (0.50)
  blocking collectives: 231 us -> 50.9 us
  local copies, waits for them, and re-layouts: 110 us -> 14 us
  starting transfers between devices: 17.9 us -> 50.7 us
  Pallas kernels: 0 us -> 14.9 us
  matrix products: 16.7 us -> 2.57 us
    all_to_all x1 -> x2, blocking collectives: 187 us -> 50.9 us  [the longest x1 37.2 us: to_experts(): lax.all_to_all(buffer.reshape(experts, 2, width), 'ep', split_axis=0, con...]
    ppermute x0 -> x7, waiting for transfers between devices: none -> 69 us  [shift(): return lax.ppermute(x, 'rep', [(i, (i + by) % nrep) for i in range(nrep)])]
    all_gather x2 -> x0, blocking collectives: 44.4 us -> none  [the longest x1 25.3 us: per_device(): lax.all_gather(dest, 'rep', axis=0, tiled=True)]
    all_gather x1, waiting for transfers between devices: 40.6 us -> 0.01 us  [per_device(): lax.all_gather(jnp.swapaxes(down_weight[0], 0, 1), 'rep', axis=0, tiled=T...]
    gather x2 -> x0, local copies, waits for them, and re-layouts: 32.7 us -> none  [the longest x1 32.1 us: fill_slots(): return padded[owner]]
    reshape x8 -> x10, local copies, waits for them, and re-layouts: 41.2 us -> 9.1 us  [the longest x2 3.55 us: to_experts(): return moved.reshape(slots, width)]
    ppermute x0 -> x7, starting transfers between devices: none -> 30.4 us  [shift(): return lax.ppermute(x, 'rep', [(i, (i + by) % nrep) for i in range(nrep)])]
    all_to_all x2, waiting for transfers between devices: 48 us -> 22.6 us  [the longest x1 22.6 us: per_device(): lax.all_to_all(expert_out.reshape(experts, 2, width), 'ep', split_axis=0,...]
  transfers between devices with their start and end apart: 3 -> 10, of which waited for: 3 -> 5; matrix products, arithmetic and copies ran while one was open for 1% -> 5% of each run, Pallas kernels for 0% -> 3%
where the time goes in v1:
time: 243 us; the launch traced here: 242 us
  waiting for transfers between devices  92.3 us (38%)
  blocking collectives  50.9 us (21%)
  starting transfers between devices  50.7 us (21%)
  Pallas kernels  14.9 us (6%)
  between operations  14.3 us (6%)
  local copies, waits for them, and re-layouts  14 us (6%)
  matrix products  2.57 us (1%)
    ppermute x7, waiting for transfers between devices, shift(): return lax.ppermute(x, 'rep', [(i, (i + by) % nrep) for i in range(nrep)])  69 us
    all_to_all x1, blocking collectives, to_experts(): lax.all_to_all(buffer.reshape(experts, 2, width), 'ep', split_axis=0, con...  37.2 us
    ppermute x7, starting transfers between devices, shift(): return lax.ppermute(x, 'rep', [(i, (i + by) % nrep) for i in range(nrep)])  30.4 us
    all_to_all x1, waiting for transfers between devices, per_device(): lax.all_to_all(expert_out.reshape(experts, 2, width), 'ep', split_axis=0,...  22.6 us
    all_to_all x1, blocking collectives, per_device(): lax.all_to_all(by_home, 'rep', split_axis=0, concat_axis=0, tiled=True)  13.7 us
    all_to_all x1, starting transfers between devices, per_device(): lax.all_to_all(expert_out.reshape(experts, 2, width), 'ep', split_axis=0,...  13.4 us
    pallas_call x1, Pallas kernels, per_device(): pl.pallas_call(down_kernel, out_shape=jax.ShapeDtypeStruct((slots, width)...  6.95 us
    all_to_all x1, starting transfers between devices, to_experts(): lax.all_to_all(buffer.reshape(experts, 2, width), 'ep', split_axis=0, con...  6.82 us
  transfers between devices with their start and end apart: 10, of which 5 were waited for; matrix products, arithmetic and copies ran while one was open for 5% of the time, Pallas kernels for 3%

profile of v1, /device:TPU:1, one launch (start us, length us, event | category | flops | bytes accessed | tf_op | source)
XLA Modules:
  0.0 241.7 jit_solution(1385063084373438717)
XLA Ops:
  7.2 0.7 all-gather.2.cloned.1.call-update
  7.9 0.7 copy.27
  8.8 0.8 reshape.85.hidden_ref
  9.7 0.7 reshape.86.gain_ref
  11.1 0.7 copy-done.5
  12.7 37.2 %all_to_all.20 = bf16[64,2,3584]{2,1,0:T(2,128)(2,1)S(1)} all-to-all(bf16[64,2,3584]{2,1,0:T(2,128)(2,1)S(1)} %reshape.91), channel_id=1, replica_groups=mesh['rep'=8,'ep'=64] {'ep'}, dimensions={0} | all-to-all | bytes 1835008 | tf_op jit(solution)/shard_map/all_to_all | solution.py:184
  50.2 4.0 %collective-permute-start = (bf16[128,3584]{1,0:T(8,128)(2,1)S(1)}, bf16[128,3584]{1,0:T(8,128)(2,1)S(1)}, u32[]{:S(2)}, u32[]{:S(2)}) collective-permute-start(bf16[128,3584]{1,0:T(8,128)(2,1)S(1)} %reshape.92.refs_0_), channel_id=1, source_target_pairs={{0,64},{64,128},{128,192},{192,256},{256,320},{320,384},{384,448},... | collective-permute-start | bytes 2752520 | tf_op jit(solution)/shard_map/ppermute | solution.py:190
  54.2 8.6 %collective-permute-start.3 = (bf16[128,3584]{1,0:T(8,128)(2,1)S(1)}, bf16[128,3584]{1,0:T(8,128)(2,1)}, u32[]{:S(2)}, u32[]{:S(2)}) collective-permute-start(bf16[128,3584]{1,0:T(8,128)(2,1)S(1)} %reshape.92.refs_0_), channel_id=1, source_target_pairs={{0,448},{64,0},{128,64},{192,128},{256,192},{320,256},{384,320},{4... | collective-permute-start | bytes 2752520 | tf_op jit(solution)/shard_map/ppermute | solution.py:190
  62.8 4.5 %collective-permute-start.6 = (bf16[8,3712]{1,0:T(8,128)(2,1)S(1)}, bf16[8,3712]{1,0:T(8,128)(2,1)S(1)}, u32[]{:S(2)}, u32[]{:S(2)}) collective-permute-start(bf16[8,3712]{1,0:T(8,128)(2,1)S(1)} %get-tuple-element.5.rows_ref), channel_id=1, source_target_pairs={{0,256},{64,320},{128,384},{192,448},{256,0},{320,64},{384,128},{4... | collective-permute-start | bytes 178184 | tf_op jit(solution)/shard_map/ppermute | solution.py:190
  67.3 38.7 %collective-permute-done.6.rows_ref = bf16[8,3712]{1,0:T(8,128)(2,1)S(1)} collective-permute-done((bf16[8,3712]{1,0:T(8,128)(2,1)S(1)}, bf16[8,3712]{1,0:T(8,128)(2,1)S(1)}, u32[]{:S(2)}, u32[]{:S(2)}) %collective-permute-start.6) | collective-permute-done | bytes 59424 | tf_op jit(solution)/shard_map/ppermute | solution.py:190
  106.5 1.3 reshape.93
  107.8 6.8 %all-to-all-start.1 = ((bf16[64,2,3584]{2,1,0:T(2,128)(2,1)}), bf16[64,2,3584]{2,1,0:T(2,128)(2,1)}, u32[]{:S(2)}, u32[]{:S(2)}) async-start(bf16[64,2,3584]{2,1,0:T(2,128)(2,1)} %reshape.93), calls=%async_computation.1 | async-start | bytes 1835008 | tf_op jit(solution)/shard_map/all_to_all | solution.py:184
  114.6 4.8 %collective-permute-start.1 = (bf16[128,3584]{1,0:T(8,128)(2,1)S(1)}, bf16[128,3584]{1,0:T(8,128)(2,1)}, u32[]{:S(2)}, u32[]{:S(2)}) collective-permute-start(bf16[128,3584]{1,0:T(8,128)(2,1)S(1)} %collective-permute-done.refs_0_), channel_id=1, source_target_pairs={{0,64},{64,128},{128,192},{192,256},{256,320},{320,384},{384,448},... | collective-permute-start | bytes 2752520 | tf_op jit(solution)/shard_map/ppermute | solution.py:190
  119.4 1.0 copy-done.2
  120.4 2.0 collective-permute-start.4
  122.4 22.4 %collective-permute-done.1.refs_0_ = bf16[128,3584]{1,0:T(8,128)(2,1)} collective-permute-done((bf16[128,3584]{1,0:T(8,128)(2,1)S(1)}, bf16[128,3584]{1,0:T(8,128)(2,1)}, u32[]{:S(2)}, u32[]{:S(2)}) %collective-permute-start.1) | collective-permute-done | bytes 917536 | tf_op jit(solution)/shard_map/ppermute | solution.py:190
  144.7 1.9 collective-permute-start.2
  146.7 4.6 %collective-permute-start.5 = (bf16[128,3584]{1,0:T(8,128)(2,1)}, bf16[128,3584]{1,0:T(8,128)(2,1)}, u32[]{:S(2)}, u32[]{:S(2)}) collective-permute-start(bf16[128,3584]{1,0:T(8,128)(2,1)} %collective-permute-done.4.refs_1_), channel_id=1, source_target_pairs={{0,448},{64,0},{128,64},{192,128},{256,192},{320,256},{384,320},{4... | collective-permute-start | bytes 2752520 | tf_op jit(solution)/shard_map/ppermute | solution.py:190
  151.3 1.7 pad_maximum_fusion.weight_ref
  152.9 3.2 %reshape.94.refs_1_ = bf16[128,3584]{1,0:T(8,128)(2,1)} reshape(bf16[64,2,3584]{2,1,0:T(2,128)(2,1)} %all-to-all-done.1) | data formatting | bytes 1835008 | tf_op jit(solution)/shard_map/reshape | solution.py:187
  156.1 1.2 copy-done.1
  158.5 1.9 inner.3.refs_2_
  160.4 2.1 inner.4.refs_3_
  162.5 6.9 %collective-permute-done.2.refs_0_ = bf16[128,3584]{1,0:T(8,128)(2,1)} collective-permute-done((bf16[128,3584]{1,0:T(8,128)(2,1)}, bf16[128,3584]{1,0:T(8,128)(2,1)}, u32[]{:S(2)}, u32[]{:S(2)}) %collective-permute-start.2) | collective-permute-done | bytes 917536 | tf_op jit(solution)/shard_map/ppermute | solution.py:190
  169.4 0.9 collective-permute-done.5.refs_1_
  170.3 2.1 last_inner.1
  172.4 13.7 %all_to_all.21.inner_ref = bf16[8,128,128]{2,1,0:T(8,128)(2,1)S(1)} all-to-all(bf16[8,128,128]{2,1,0:T(8,128)(2,1)S(1)} %last_inner.1), channel_id=1, replica_groups=mesh['rep'=8,'ep'=64] {'rep'}, dimensions={0} | all-to-all | bytes 524288 | tf_op jit(solution)/shard_map/all_to_all | solution.py:235
  186.2 6.9 %down.1 = bf16[128,3584]{1,0:T(8,128)(2,1)S(1)} custom-call(bf16[8,128,128]{2,1,0:T(8,128)(2,1)S(1)} %all_to_all.21.inner_ref, bf16[3584,1024]{1,0:T(8,128)(2,1)} %all-gather.2.cloned.1.call-done.weight_ref), custom_call_target="tpu_custom_call" | custom-call | tf_op jit(solution)/shard_map/down/pallas_call | solution.py:237
  193.2 1.3 reshape.95
  194.4 13.4 %all-to-all-start.3 = ((bf16[64,2,3584]{2,1,0:T(2,128)(2,1)}), bf16[64,2,3584]{2,1,0:T(2,128)(2,1)S(1)}, u32[]{:S(2)}, u32[]{:S(2)}) async-start(bf16[64,2,3584]{2,1,0:T(2,128)(2,1)} %reshape.95), calls=%async_computation.3 | async-start | bytes 1835008 | tf_op jit(solution)/shard_map/all_to_all | solution.py:249
  209.9 1.2 fusion.1
  211.0 22.6 %all-to-all-done.3 = bf16[64,2,3584]{2,1,0:T(2,128)(2,1)S(1)} async-done(((bf16[64,2,3584]{2,1,0:T(2,128)(2,1)}), bf16[64,2,3584]{2,1,0:T(2,128)(2,1)S(1)}, u32[]{:S(2)}, u32[]{:S(2)}) %all-to-all-start.3) | async-done | bytes 917536 | tf_op jit(solution)/shard_map/all_to_all | solution.py:249
  (45 shorter events, 6.9 us)
Async XLA Ops:
  7.2 200.9 %copy-start = (bf16[4,2,64,576]{3,2,1,0:T(8,128)(2,1)S(1)}, bf16[4,2,64,576]{3,2,1,0:T(8,128)(2,1)}, u32[]{:S(2)}) copy-start(bf16[4,2,64,576]{3,2,1,0:T(8,128)(2,1)} %param.12) | copy-start | bytes 1769476
  7.2 179.0 %all-gather.2.cloned.1.call-start = ((), (), s32[]{:S(2)}) async-start(), calls=%async_computation.4 | async-start | bytes 8257536 | tf_op jit(solution)/shard_map/all_gather | solution.py:154
  10.4 0.7 copy-start.4
  11.1 0.7 copy-start.5
  50.2 64.4 %collective-permute-start = (bf16[128,3584]{1,0:T(8,128)(2,1)S(1)}, bf16[128,3584]{1,0:T(8,128)(2,1)S(1)}, u32[]{:S(2)}, u32[]{:S(2)}) collective-permute-start(bf16[128,3584]{1,0:T(8,128)(2,1)S(1)} %reshape.92.refs_0_), channel_id=1, source_target_pairs={{0,64},{64,128},{128,192},{192,256},{256,320},{320,384},{384,448},... | collective-permute-start | bytes 2752520 | tf_op jit(solution)/shard_map/ppermute | solution.py:190
  54.2 66.2 %collective-permute-start.3 = (bf16[128,3584]{1,0:T(8,128)(2,1)S(1)}, bf16[128,3584]{1,0:T(8,128)(2,1)}, u32[]{:S(2)}, u32[]{:S(2)}) collective-permute-start(bf16[128,3584]{1,0:T(8,128)(2,1)S(1)} %reshape.92.refs_0_), channel_id=1, source_target_pairs={{0,448},{64,0},{128,64},{192,128},{256,192},{320,256},{384,320},{4... | collective-permute-start | bytes 2752520 | tf_op jit(solution)/shard_map/ppermute | solution.py:190
  62.8 43.3 %collective-permute-start.6 = (bf16[8,3712]{1,0:T(8,128)(2,1)S(1)}, bf16[8,3712]{1,0:T(8,128)(2,1)S(1)}, u32[]{:S(2)}, u32[]{:S(2)}) collective-permute-start(bf16[8,3712]{1,0:T(8,128)(2,1)S(1)} %get-tuple-element.5.rows_ref), channel_id=1, source_target_pairs={{0,256},{64,320},{128,384},{192,448},{256,0},{320,64},{384,128},{4... | collective-permute-start | bytes 178184 | tf_op jit(solution)/shard_map/ppermute | solution.py:190
  107.8 45.1 %all-to-all-start.1 = ((bf16[64,2,3584]{2,1,0:T(2,128)(2,1)}), bf16[64,2,3584]{2,1,0:T(2,128)(2,1)}, u32[]{:S(2)}, u32[]{:S(2)}) async-start(bf16[64,2,3584]{2,1,0:T(2,128)(2,1)} %reshape.93), calls=%async_computation.1 | async-start | bytes 1835008 | tf_op jit(solution)/shard_map/all_to_all | solution.py:184
  114.6 30.1 %collective-permute-start.1 = (bf16[128,3584]{1,0:T(8,128)(2,1)S(1)}, bf16[128,3584]{1,0:T(8,128)(2,1)}, u32[]{:S(2)}, u32[]{:S(2)}) collective-permute-start(bf16[128,3584]{1,0:T(8,128)(2,1)S(1)} %collective-permute-done.refs_0_), channel_id=1, source_target_pairs={{0,64},{64,128},{128,192},{192,256},{256,320},{320,384},{384,448},... | collective-permute-start | bytes 2752520 | tf_op jit(solution)/shard_map/ppermute | solution.py:190
  119.4 1.0 copy-start.2
  120.4 26.3 %collective-permute-start.4 = (bf16[128,3584]{1,0:T(8,128)(2,1)}, bf16[128,3584]{1,0:T(8,128)(2,1)}, u32[]{:S(2)}, u32[]{:S(2)}) collective-permute-start(bf16[128,3584]{1,0:T(8,128)(2,1)} %collective-permute-done.3.refs_1_), channel_id=1, source_target_pairs={{0,448},{64,0},{128,64},{192,128},{256,192},{320,256},{384,320},{4... | collective-permute-start | bytes 2752520 | tf_op jit(solution)/shard_map/ppermute | solution.py:190
  144.7 24.7 %collective-permute-start.2 = (bf16[128,3584]{1,0:T(8,128)(2,1)}, bf16[128,3584]{1,0:T(8,128)(2,1)}, u32[]{:S(2)}, u32[]{:S(2)}) collective-permute-start(bf16[128,3584]{1,0:T(8,128)(2,1)} %collective-permute-done.1.refs_0_), channel_id=1, source_target_pairs={{0,64},{64,128},{128,192},{192,256},{256,320},{320,384},{384,448},... | collective-permute-start | bytes 2752520 | tf_op jit(solution)/shard_map/ppermute | solution.py:190
  146.7 23.6 %collective-permute-start.5 = (bf16[128,3584]{1,0:T(8,128)(2,1)}, bf16[128,3584]{1,0:T(8,128)(2,1)}, u32[]{:S(2)}, u32[]{:S(2)}) collective-permute-start(bf16[128,3584]{1,0:T(8,128)(2,1)} %collective-permute-done.4.refs_1_), channel_id=1, source_target_pairs={{0,448},{64,0},{128,64},{192,128},{256,192},{320,256},{384,320},{4... | collective-permute-start | bytes 2752520 | tf_op jit(solution)/shard_map/ppermute | solution.py:190
  156.1 1.2 copy-start.1
  157.3 1.2 copy-start.3
  193.1 14.8 %copy-start.8 = (s32[4]{0:T(128)S(1)}, s32[4]{0:T(128)}, u32[]{:S(2)}) copy-start(s32[4]{0:T(128)} %param.16) | copy-start | bytes 52
  193.1 14.9 %copy-start.9 = (s32[4]{0:T(128)S(1)}, s32[4]{0:T(128)}, u32[]{:S(2)}) copy-start(s32[4]{0:T(128)} %param.15) | copy-start | bytes 52
  193.1 14.9 %copy-start.7 = (bf16[4,2,576]{2,1,0:T(2,128)(2,1)S(1)}, bf16[4,2,576]{2,1,0:T(2,128)(2,1)}, u32[]{:S(2)}) copy-start(bf16[4,2,576]{2,1,0:T(2,128)(2,1)} %param.14) | copy-start | bytes 27652
  193.2 15.4 %copy-start.6 = (bf16[4,256,576]{1,2,0:T(8,128)(2,1)S(1)}, bf16[4,256,576]{1,2,0:T(8,128)(2,1)}, u32[]{:S(2)}) copy-start(bf16[4,256,576]{1,2,0:T(8,128)(2,1)} %param.13) | copy-start | bytes 3538948
  194.4 39.2 %all-to-all-start.3 = ((bf16[64,2,3584]{2,1,0:T(2,128)(2,1)}), bf16[64,2,3584]{2,1,0:T(2,128)(2,1)S(1)}, u32[]{:S(2)}, u32[]{:S(2)}) async-start(bf16[64,2,3584]{2,1,0:T(2,128)(2,1)} %reshape.95), calls=%async_computation.3 | async-start | bytes 1835008 | tf_op jit(solution)/shard_map/all_to_all | solution.py:249
Sparse Core Ops, SparseCore 0:
  10.1 119.4 all-gather.1

commit v2 on v1

--- a/solution.py
+++ b/solution.py
@@ -10,7 +10,6 @@
 LATENT_WIDTH = 512
 
 score_scale = 192.0 ** (-0.5)
-SMEM = pl.BlockSpec(memory_space=pltpu.SMEM)
 VMEM = pl.BlockSpec(memory_space=pltpu.VMEM)
 limit = pltpu.CompilerParams(vmem_limit_bytes=48 * 1024 * 1024)
 
@@ -60,34 +59,50 @@
     return (g / (1.0 + jnp.exp(-g)) * u).astype(jnp.bfloat16)
 
 
-def inner_kernel(weight_ref, *refs):
+def inner_kernel(have, weight_ref, *refs):
+    out_ref = refs[-1]
+    at = 0
+    for ref in refs[:have]:
+        for i in range(ref.shape[0]):
+            out_ref[at] = ref[i]
+            at += 1
+    for rows_ref in refs[have:-1]:
+        out_ref[at] = inner_piece(rows_ref[...], weight_ref[...])
+        at += 1
+
+
+def last_inner_kernel(weight_ref, *refs):
     out_ref = refs[-1]
     for i, rows_ref in enumerate(refs[:-1]):
-        out_ref[i] = inner_piece(rows_ref[...], weight_ref[...])
-
-
-def last_inner_kernel(places, me_ref, weight_ref, *refs):
-    out_ref = refs[-1]
-    count = out_ref.shape[0]
-    new, old = refs[:2], refs[2:-1]
-    for place, rows_ref in zip(places[:2], new):
-        out_ref[lax.rem(me_ref[0] + place + count, count)] = inner_piece(
-            rows_ref[...], weight_ref[...]
-        )
-    for i, place in enumerate(places[2:]):
-        out_ref[lax.rem(me_ref[0] + place + count, count)] = old[i // 2][i % 2]
-
-
-def down_kernel(inner_ref, weight_ref, out_ref):
-    full = jnp.concatenate([inner_ref[r] for r in range(inner_ref.shape[0])], axis=1)
-    out_ref[...] = lax.dot_general(
-        full, weight_ref[...], (((1,), (1,)), ((), ())), preferred_element_type=jnp.float32
-    ).astype(jnp.bfloat16)
+        piece = inner_piece(rows_ref[...], weight_ref[...])
+        for r in range(out_ref.shape[0]):
+            out_ref[r, i] = piece
+
+
+def down_kernel(first_places, last_places, first_ref, last_ref, weight_ref, out_ref):
+    count, slots = first_ref.shape[0], first_ref.shape[2]
+
+    def piece(r, home):
+        place = (home - r) % count
+        if place in first_places:
+            return first_ref[r, first_places.index(place)]
+        return last_ref[r, last_places.index(place)]
+
+    for home in range(count):
+        full = jnp.concatenate([piece(r, home) for r in range(count)], axis=1)
+        out_ref[home * slots : (home + 1) * slots, :] = lax.dot_general(
+            full, weight_ref[...], (((1,), (1,)), ((), ())), preferred_element_type=jnp.float32
+        ).astype(jnp.bfloat16)
 
 
 def mix_kernel(mix_ref, back_ref, out_ref):
-    out_ref[...] = jnp.dot(
-        mix_ref[...], back_ref[...], preferred_element_type=jnp.float32
+    mix = mix_ref[...]
+    out_ref[...] = jnp.concatenate(
+        [
+            jnp.dot(mix, back_ref[c], preferred_element_type=jnp.float32)
+            for c in range(back_ref.shape[0])
+        ],
+        axis=1,
     ).astype(jnp.bfloat16)
 
 
@@ -147,13 +162,10 @@
     experts = lax.axis_size("ep")
     rows = nreq * 2
     units = gate_weight.shape[2]
+    part = width // nrep
     slots = 2 * experts
     row_live = jnp.stack([jnp.ones_like(accepted), accepted], 1)
-    attended = attend(queries, latent_key_cache, fresh_latent_keys, lengths, row_live)
-
-    all_down = lax.all_gather(
-        jnp.swapaxes(down_weight[0], 0, 1), "rep", axis=0, tiled=True
-    )
+
     tagged, mix = pl.pallas_call(
         prepare_kernel,
         out_shape=(
@@ -172,31 +184,33 @@
         row_live.reshape(rows, 1),
     )
 
-    def to_experts(rows_in):
-        buffer = pl.pallas_call(
+    def dispatch(rows_in):
+        return pl.pallas_call(
             dispatch_kernel,
             out_shape=jax.ShapeDtypeStruct((slots, width), jnp.bfloat16),
             in_specs=[VMEM],
             out_specs=VMEM,
             compiler_params=limit,
             name="dispatch",
-        )(rows_in)
-        moved = lax.all_to_all(
-            buffer.reshape(experts, 2, width), "ep", split_axis=0, concat_axis=0, tiled=True
+        )(rows_in).reshape(experts, 2, width)
+
+    def to_experts(buffer):
+        return lax.all_to_all(buffer, "ep", split_axis=0, concat_axis=0, tiled=True).reshape(
+            slots, width
         )
-        return moved.reshape(slots, width)
 
     def shift(x, by):
         return lax.ppermute(x, "rep", [(i, (i + by) % nrep) for i in range(nrep)])
 
     both_weight = jnp.concatenate([gate_weight[0], up_weight[0]], axis=1)
 
-    def inner_blocks(*blocks):
+    def inner_blocks(before, *blocks):
         n = len(blocks)
+        count = n + sum(piece.shape[0] for piece in before)
         return pl.pallas_call(
-            inner_kernel,
-            out_shape=jax.ShapeDtypeStruct((n, slots, units), jnp.bfloat16),
-            in_specs=[VMEM] * (n + 1),
+            partial(inner_kernel, len(before)),
+            out_shape=jax.ShapeDtypeStruct((count, slots, units), jnp.bfloat16),
+            in_specs=[VMEM] * (1 + len(before) + n),
             out_specs=VMEM,
             compiler_params=limit,
             cost_estimate=pl.CostEstimate(
@@ -205,50 +219,47 @@
                 transcendentals=n * slots * units,
             ),
             name="inner",
-        )(both_weight, *blocks)
-
-    own = to_experts(tagged)
-    far = to_experts(shift(tagged, nrep // 2))
-    places, done = [], []
-    up_block = down_block = own
-    for s in range(1, nrep // 2):
-        up_block, down_block = shift(up_block, 1), shift(down_block, -1)
-        places = places + [-s, s]
-        if s < nrep // 2 - 1:
-            done.append(inner_blocks(up_block, down_block))
-    places = places[-2:] + places[:-2] + [0, nrep // 2]
-    done.append(inner_blocks(own, far))
-    by_home = pl.pallas_call(
-        partial(last_inner_kernel, places),
-        out_shape=jax.ShapeDtypeStruct((nrep, slots, units), jnp.bfloat16),
-        in_specs=[SMEM] + [VMEM] * (3 + len(done)),
+        )(both_weight, *before, *blocks)
+
+    half = nrep // 2
+    far_rows = shift(tagged, half)
+    own = to_experts(dispatch(tagged))
+    own, far_buffer = lax.optimization_barrier((own, dispatch(far_rows)))
+    far = to_experts(far_buffer)
+    up_one, down_one = shift(own, 1), shift(own, -1)
+    near = inner_blocks([], own, up_one, down_one)
+    up_two, down_two = shift(up_one, 1), shift(down_one, -1)
+    up_far, down_far = shift(far, 1), shift(far, -1)
+    first_places = [0, nrep - 1, 1, half, nrep - 2, 2]
+    first = inner_blocks([near], far, up_two, down_two)
+    first = lax.all_gather(first, "rep", axis=0, tiled=False)
+    last_places = [half - 1, half + 1]
+    last = pl.pallas_call(
+        last_inner_kernel,
+        out_shape=jax.ShapeDtypeStruct((nrep, 2, slots, units), jnp.bfloat16),
+        in_specs=[VMEM] * 3,
         out_specs=VMEM,
         compiler_params=limit,
         name="last_inner",
-    )(
-        lax.axis_index("rep").astype(jnp.int32).reshape(1),
-        both_weight,
-        up_block,
-        down_block,
-        *done,
-    )
-    inner = lax.all_to_all(by_home, "rep", split_axis=0, concat_axis=0, tiled=True)
-    columns = 512
+    )(both_weight, up_far, down_far)
+    last = lax.all_to_all(last, "rep", split_axis=0, concat_axis=0, tiled=True)
     expert_out = pl.pallas_call(
-        down_kernel,
-        out_shape=jax.ShapeDtypeStruct((slots, width), jnp.bfloat16),
-        grid=(width // columns,),
-        in_specs=[
-            pl.BlockSpec((nrep, slots, units), lambda i: (0, 0, 0)),
-            pl.BlockSpec((columns, nrep * units), lambda i: (i, 0)),
-        ],
-        out_specs=pl.BlockSpec((slots, columns), lambda i: (0, i)),
+        partial(down_kernel, first_places, last_places),
+        out_shape=jax.ShapeDtypeStruct((nrep * slots, part), jnp.bfloat16),
+        in_specs=[VMEM] * 3,
+        out_specs=VMEM,
         compiler_params=limit,
         name="down",
-    )(inner, all_down)
+    )(first, last, jnp.swapaxes(down_weight[0], 0, 1))
+    queries, expert_out = lax.optimization_barrier((queries, expert_out))
+    attended = attend(queries, latent_key_cache, fresh_latent_keys, lengths, row_live)
     back = lax.all_to_all(
-        expert_out.reshape(experts, 2, width), "ep", split_axis=0, concat_axis=0, tiled=True
-    ).reshape(slots, width)
+        expert_out.reshape(nrep * experts, 2, part),
+        ("rep", "ep"),
+        split_axis=0,
+        concat_axis=0,
+        tiled=True,
+    ).reshape(nrep, slots, part)
     routed = pl.pallas_call(
         mix_kernel,
         out_shape=jax.ShapeDtypeStruct((rows, width), jnp.bfloat16),

time: 243 us -> 231 us (0.951)
  blocking collectives: 50.9 us -> 16.9 us
  starting transfers between devices: 50.7 us -> 73.9 us
  Pallas kernels: 14.9 us -> 8.91 us
  waiting for transfers between devices: 92.3 us -> 97 us
    all_to_all x2 -> x1, blocking collectives: 50.9 us -> 16.9 us  [per_device(): last = lax.all_to_all(last, 'rep', split_axis=0, concat_axis=0, tiled=True)]
    all_to_all x2 -> x3, waiting for transfers between devices: 22.6 us -> 45.3 us  [the longest x1 30.5 us: per_device(): lax.all_to_all(expert_out.reshape(nrep * experts, 2, part), ('rep', 'ep')...]
    ppermute x7, waiting for transfers between devices: 69 us -> 51.8 us  [shift(): return lax.ppermute(x, 'rep', [(i, (i + by) % nrep) for i in range(nrep)])]
    all_to_all x2 -> x3, starting transfers between devices: 20.3 us -> 36.9 us  [the longest x1 18.6 us: per_device(): lax.all_to_all(expert_out.reshape(nrep * experts, 2, part), ('rep', 'ep')...]
    ppermute x7, starting transfers between devices: 30.4 us -> 36.9 us  [shift(): return lax.ppermute(x, 'rep', [(i, (i + by) % nrep) for i in range(nrep)])]
    pallas_call x7 -> x6, Pallas kernels: 14.6 us -> 8.48 us  [the longest x2 4.72 us: inner_blocks(): pl.pallas_call(partial(inner_kernel, len(before)), out_shape=jax.ShapeDty...]
  transfers between devices with their start and end apart: 10 -> 11, of which waited for: 5 -> 9; matrix products, arithmetic and copies ran while one was open for 5% -> 4% of each run, Pallas kernels for 3% -> 2%
where the time goes in v2:
time: 231 us; the launch traced here: 230 us
  waiting for transfers between devices  97 us (42%)
  starting transfers between devices  73.9 us (32%)
  blocking collectives  16.9 us (7%)
  local copies, waits for them, and re-layouts  14.3 us (6%)
  between operations  14.3 us (6%)
  Pallas kernels  8.91 us (4%)
  matrix products  2.57 us (1%)
    ppermute x7, waiting for transfers between devices, shift(): return lax.ppermute(x, 'rep', [(i, (i + by) % nrep) for i in range(nrep)])  51.8 us
    ppermute x7, starting transfers between devices, shift(): return lax.ppermute(x, 'rep', [(i, (i + by) % nrep) for i in range(nrep)])  36.9 us
    all_to_all x1, waiting for transfers between devices, per_device(): lax.all_to_all(expert_out.reshape(nrep * experts, 2, part), ('rep', 'ep')...  30.5 us
    all_to_all x1, starting transfers between devices, per_device(): lax.all_to_all(expert_out.reshape(nrep * experts, 2, part), ('rep', 'ep')...  18.6 us
    all_to_all x2, starting transfers between devices, to_experts(): lax.all_to_all(buffer, 'ep', split_axis=0, concat_axis=0, tiled=True)  18.3 us
    all_to_all x1, blocking collectives, per_device(): last = lax.all_to_all(last, 'rep', split_axis=0, concat_axis=0, tiled=True)  16.9 us
    all_to_all x2, waiting for transfers between devices, to_experts(): lax.all_to_all(buffer, 'ep', split_axis=0, concat_axis=0, tiled=True)  14.8 us
    pallas_call x2, Pallas kernels, inner_blocks(): pl.pallas_call(partial(inner_kernel, len(before)), out_shape=jax.ShapeDty...  4.72 us
  transfers between devices with their start and end apart: 11, of which 9 were waited for; matrix products, arithmetic and copies ran while one was open for 4% of the time, Pallas kernels for 2%

profile of v2, /device:TPU:1, one launch (start us, length us, event | category | flops | bytes accessed | tf_op | source)
XLA Modules:
  0.0 229.9 jit_solution(13419731929904871397)
XLA Ops:
  8.1 0.8 reshape.82.hidden_ref
  11.6 1.3 reshape.87
  12.9 11.6 %all-to-all-start = ((bf16[64,2,3584]{2,1,0:T(2,128)(2,1)}), bf16[64,2,3584]{2,1,0:T(2,128)(2,1)S(1)}, u32[]{:S(2)}, u32[]{:S(2)}) async-start(bf16[64,2,3584]{2,1,0:T(2,128)(2,1)} %reshape.87), calls=%async_computation | async-start | bytes 1835008 | tf_op jit(solution)/shard_map/all_to_all | solution.py:198
  24.5 10.6 %collective-permute-start = (bf16[8,3712]{1,0:T(8,128)(2,1)S(1)}, bf16[8,3712]{1,0:T(8,128)(2,1)S(1)}, u32[]{:S(2)}, u32[]{:S(2)}) collective-permute-start(bf16[8,3712]{1,0:T(8,128)(2,1)S(1)} %get-tuple-element.8.rows_ref), channel_id=1, source_target_pairs={{0,256},{64,320},{128,384},{192,448},{256,0},{320,64},{384,128},{4... | collective-permute-start | bytes 178184 | tf_op jit(solution)/shard_map/ppermute | solution.py:203
  35.2 1.9 collective-permute-done.rows_ref
  37.5 1.3 reshape.89
  38.7 11.5 %all-to-all-done = bf16[64,2,3584]{2,1,0:T(2,128)(2,1)S(1)} async-done(((bf16[64,2,3584]{2,1,0:T(2,128)(2,1)}), bf16[64,2,3584]{2,1,0:T(2,128)(2,1)S(1)}, u32[]{:S(2)}, u32[]{:S(2)}) %all-to-all-start) | async-done | bytes 917536 | tf_op jit(solution)/shard_map/all_to_all | solution.py:198
  50.6 4.0 %collective-permute-start.1 = (bf16[128,3584]{1,0:T(8,128)(2,1)S(1)}, bf16[128,3584]{1,0:T(8,128)(2,1)}, u32[]{:S(2)}, u32[]{:S(2)}) collective-permute-start(bf16[128,3584]{1,0:T(8,128)(2,1)S(1)} %reshape.88.refs_0_), channel_id=1, source_target_pairs={{0,64},{64,128},{128,192},{192,256},{256,320},{320,384},{384,448},... | collective-permute-start | bytes 2752520 | tf_op jit(solution)/shard_map/ppermute | solution.py:203
  54.6 8.6 %collective-permute-start.2 = (bf16[128,3584]{1,0:T(8,128)(2,1)S(1)}, bf16[128,3584]{1,0:T(8,128)(2,1)}, u32[]{:S(2)}, u32[]{:S(2)}) collective-permute-start(bf16[128,3584]{1,0:T(8,128)(2,1)S(1)} %reshape.88.refs_0_), channel_id=1, source_target_pairs={{0,448},{64,0},{128,64},{192,128},{256,192},{320,256},{384,320},{4... | collective-permute-start | bytes 2752520 | tf_op jit(solution)/shard_map/ppermute | solution.py:203
  63.2 6.7 %all-to-all-start.1 = ((bf16[64,2,3584]{2,1,0:T(2,128)(2,1)}), bf16[64,2,3584]{2,1,0:T(2,128)(2,1)}, u32[]{:S(2)}, u32[]{:S(2)}) async-start(bf16[64,2,3584]{2,1,0:T(2,128)(2,1)} %reshape.89), calls=%async_computation.1 | async-start | bytes 1835008 | tf_op jit(solution)/shard_map/all_to_all | solution.py:198
  70.0 11.9 %collective-permute-done.1.refs_1_ = bf16[128,3584]{1,0:T(8,128)(2,1)} collective-permute-done((bf16[128,3584]{1,0:T(8,128)(2,1)S(1)}, bf16[128,3584]{1,0:T(8,128)(2,1)}, u32[]{:S(2)}, u32[]{:S(2)}) %collective-permute-start.1) | collective-permute-done | bytes 917536 | tf_op jit(solution)/shard_map/ppermute | solution.py:203
  81.9 1.9 collective-permute-start.3
  83.8 4.6 %collective-permute-start.4 = (bf16[128,3584]{1,0:T(8,128)(2,1)}, bf16[128,3584]{1,0:T(8,128)(2,1)}, u32[]{:S(2)}, u32[]{:S(2)}) collective-permute-start(bf16[128,3584]{1,0:T(8,128)(2,1)} %collective-permute-done.2.refs_2_), channel_id=1, source_target_pairs={{0,448},{64,0},{128,64},{192,128},{256,192},{320,256},{384,320},{4... | collective-permute-start | bytes 2752520 | tf_op jit(solution)/shard_map/ppermute | solution.py:203
  88.4 1.7 pad_maximum_fusion.weight_ref
  90.0 2.4 %inner.2.refs_0_ = bf16[3,128,128]{2,1,0:T(8,128)(2,1)S(1)} custom-call(bf16[3584,256]{1,0:T(8,128)(2,1)S(1)} %pad_maximum_fusion.weight_ref, bf16[128,3584]{1,0:T(8,128)(2,1)S(1)} %reshape.88.refs_0_, bf16[128,3584]{1,0:T(8,128)(2,1)} %collective-permute-done.1.refs_1_, bf16[128,3584]{1,0:T(8,128)(2,1)} %collective-permute-done.2.refs_2_), custom_call_target="tpu_custom_call" | custom-call | flops 704643072 | bytes 4587520 | tf_op jit(solution)/shard_map/inner/pallas_call | solution.py:210
  92.4 3.2 %all-to-all-done.1 = bf16[64,2,3584]{2,1,0:T(2,128)(2,1)} async-done(((bf16[64,2,3584]{2,1,0:T(2,128)(2,1)}), bf16[64,2,3584]{2,1,0:T(2,128)(2,1)}, u32[]{:S(2)}, u32[]{:S(2)}) %all-to-all-start.1) | async-done | bytes 917536 | tf_op jit(solution)/shard_map/all_to_all | solution.py:198
  95.6 2.5 %reshape.90.refs_1_ = bf16[128,3584]{1,0:T(8,128)(2,1)S(1)} reshape(bf16[64,2,3584]{2,1,0:T(2,128)(2,1)} %all-to-all-done.1) | data formatting | bytes 1835008 | tf_op jit(solution)/shard_map/reshape | solution.py:198
  98.1 8.2 %collective-permute-done.3.refs_2_ = bf16[128,3584]{1,0:T(8,128)(2,1)} collective-permute-done((bf16[128,3584]{1,0:T(8,128)(2,1)}, bf16[128,3584]{1,0:T(8,128)(2,1)}, u32[]{:S(2)}, u32[]{:S(2)}) %collective-permute-start.3) | collective-permute-done | bytes 917536 | tf_op jit(solution)/shard_map/ppermute | solution.py:203
  106.3 0.9 collective-permute-done.4.refs_3_
  107.2 2.4 %inner.3 = bf16[6,128,128]{2,1,0:T(8,128)(2,1)S(1)} custom-call(bf16[3584,256]{1,0:T(8,128)(2,1)S(1)} %pad_maximum_fusion.weight_ref, bf16[3,128,128]{2,1,0:T(8,128)(2,1)S(1)} %inner.2.refs_0_, bf16[128,3584]{1,0:T(8,128)(2,1)S(1)} %reshape.90.refs_1_, bf16[128,3584]{1,0:T(8,128)(2,1)} %collective-permute-done.3.refs_2_, ...), custom_call_target="tpu_custom_call" | custom-call | flops 704643072 | bytes 4587520 | tf_op jit(solution)/shard_map/inner/pallas_call | solution.py:210
  110.3 1.9 collective-permute-start.5
  112.2 5.3 %collective-permute-start.6 = (bf16[128,3584]{1,0:T(8,128)(2,1)S(1)}, bf16[128,3584]{1,0:T(8,128)(2,1)S(1)}, u32[]{:S(2)}, u32[]{:S(2)}) collective-permute-start(bf16[128,3584]{1,0:T(8,128)(2,1)S(1)} %reshape.90.refs_1_), channel_id=1, source_target_pairs={{0,448},{64,0},{128,64},{192,128},{256,192},{320,256},{384,320},{4... | collective-permute-start | bytes 2752520 | tf_op jit(solution)/shard_map/ppermute | solution.py:203
  117.5 25.2 %collective-permute-done.5.refs_0_ = bf16[128,3584]{1,0:T(8,128)(2,1)S(1)} collective-permute-done((bf16[128,3584]{1,0:T(8,128)(2,1)S(1)}, bf16[128,3584]{1,0:T(8,128)(2,1)S(1)}, u32[]{:S(2)}, u32[]{:S(2)}) %collective-permute-start.5) | collective-permute-done | bytes 917536 | tf_op jit(solution)/shard_map/ppermute | solution.py:203
  142.7 3.8 %collective-permute-done.6.refs_1_ = bf16[128,3584]{1,0:T(8,128)(2,1)S(1)} collective-permute-done((bf16[128,3584]{1,0:T(8,128)(2,1)S(1)}, bf16[128,3584]{1,0:T(8,128)(2,1)S(1)}, u32[]{:S(2)}, u32[]{:S(2)}) %collective-permute-start.6) | collective-permute-done | bytes 917536 | tf_op jit(solution)/shard_map/ppermute | solution.py:203
  147.1 16.9 %all_to_all.20.last_ref = bf16[8,2,128,128]{3,2,1,0:T(8,128)(2,1)S(1)} all-to-all(bf16[8,2,128,128]{3,2,1,0:T(8,128)(2,1)S(1)} %last_inner.1), channel_id=1, replica_groups=mesh['rep'=8,'ep'=64] {'rep'}, dimensions={0} | all-to-all | bytes 1048576 | tf_op jit(solution)/shard_map/all_to_all | solution.py:245
  164.0 1.4 copy-done.1
  165.4 2.3 down.1
  167.7 1.3 reshape.91
  169.0 18.6 %all-to-all-start.3 = ((bf16[512,2,448]{2,1,0:T(2,128)(2,1)}), bf16[512,2,448]{2,1,0:T(2,128)(2,1)S(1)}, u32[]{:S(2)}, u32[]{:S(2)}) async-start(bf16[512,2,448]{2,1,0:T(2,128)(2,1)} %reshape.91), calls=%async_computation.3 | async-start | bytes 2097152 | tf_op jit(solution)/shard_map/all_to_all | solution.py:256
  189.6 1.2 fusion.1
  190.7 30.5 %all-to-all-done.3 = bf16[512,2,448]{2,1,0:T(2,128)(2,1)S(1)} async-done(((bf16[512,2,448]{2,1,0:T(2,128)(2,1)}), bf16[512,2,448]{2,1,0:T(2,128)(2,1)S(1)}, u32[]{:S(2)}, u32[]{:S(2)}) %all-to-all-start.3) | async-done | bytes 917536 | tf_op jit(solution)/shard_map/all_to_all | solution.py:256
  221.2 0.9 reshape.92.back_ref
  (45 shorter events, 8.7 us)
Async XLA Ops:
  7.2 180.6 %copy-start = (bf16[4,2,64,576]{3,2,1,0:T(8,128)(2,1)S(1)}, bf16[4,2,64,576]{3,2,1,0:T(8,128)(2,1)}, u32[]{:S(2)}) copy-start(bf16[4,2,64,576]{3,2,1,0:T(8,128)(2,1)} %param.12) | copy-start | bytes 1769476
  9.7 0.7 copy-start.4
  10.4 0.7 copy-start.5
  12.9 37.4 %all-to-all-start = ((bf16[64,2,3584]{2,1,0:T(2,128)(2,1)}), bf16[64,2,3584]{2,1,0:T(2,128)(2,1)S(1)}, u32[]{:S(2)}, u32[]{:S(2)}) async-start(bf16[64,2,3584]{2,1,0:T(2,128)(2,1)} %reshape.87), calls=%async_computation | async-start | bytes 1835008 | tf_op jit(solution)/shard_map/all_to_all | solution.py:198
  24.5 12.5 %collective-permute-start = (bf16[8,3712]{1,0:T(8,128)(2,1)S(1)}, bf16[8,3712]{1,0:T(8,128)(2,1)S(1)}, u32[]{:S(2)}, u32[]{:S(2)}) collective-permute-start(bf16[8,3712]{1,0:T(8,128)(2,1)S(1)} %get-tuple-element.8.rows_ref), channel_id=1, source_target_pairs={{0,256},{64,320},{128,384},{192,448},{256,0},{320,64},{384,128},{4... | collective-permute-start | bytes 178184 | tf_op jit(solution)/shard_map/ppermute | solution.py:203
  50.6 31.2 %collective-permute-start.1 = (bf16[128,3584]{1,0:T(8,128)(2,1)S(1)}, bf16[128,3584]{1,0:T(8,128)(2,1)}, u32[]{:S(2)}, u32[]{:S(2)}) collective-permute-start(bf16[128,3584]{1,0:T(8,128)(2,1)S(1)} %reshape.88.refs_0_), channel_id=1, source_target_pairs={{0,64},{64,128},{128,192},{192,256},{256,320},{320,384},{384,448},... | collective-permute-start | bytes 2752520 | tf_op jit(solution)/shard_map/ppermute | solution.py:203
  54.6 29.1 %collective-permute-start.2 = (bf16[128,3584]{1,0:T(8,128)(2,1)S(1)}, bf16[128,3584]{1,0:T(8,128)(2,1)}, u32[]{:S(2)}, u32[]{:S(2)}) collective-permute-start(bf16[128,3584]{1,0:T(8,128)(2,1)S(1)} %reshape.88.refs_0_), channel_id=1, source_target_pairs={{0,448},{64,0},{128,64},{192,128},{256,192},{320,256},{384,320},{4... | collective-permute-start | bytes 2752520 | tf_op jit(solution)/shard_map/ppermute | solution.py:203
  63.2 32.4 %all-to-all-start.1 = ((bf16[64,2,3584]{2,1,0:T(2,128)(2,1)}), bf16[64,2,3584]{2,1,0:T(2,128)(2,1)}, u32[]{:S(2)}, u32[]{:S(2)}) async-start(bf16[64,2,3584]{2,1,0:T(2,128)(2,1)} %reshape.89), calls=%async_computation.1 | async-start | bytes 1835008 | tf_op jit(solution)/shard_map/all_to_all | solution.py:198
  69.9 94.1 %all-gather.3.cloned.1.call-start = ((), (), s32[]{:S(2)}) async-start(), calls=%async_computation.4 | async-start | bytes 1769472 | tf_op jit(solution)/shard_map/all_gather | solution.py:235
  81.9 24.4 %collective-permute-start.3 = (bf16[128,3584]{1,0:T(8,128)(2,1)}, bf16[128,3584]{1,0:T(8,128)(2,1)}, u32[]{:S(2)}, u32[]{:S(2)}) collective-permute-start(bf16[128,3584]{1,0:T(8,128)(2,1)} %collective-permute-done.1.refs_1_), channel_id=1, source_target_pairs={{0,64},{64,128},{128,192},{192,256},{256,320},{320,384},{384,448},... | collective-permute-start | bytes 2752520 | tf_op jit(solution)/shard_map/ppermute | solution.py:203
  83.8 23.4 %collective-permute-start.4 = (bf16[128,3584]{1,0:T(8,128)(2,1)}, bf16[128,3584]{1,0:T(8,128)(2,1)}, u32[]{:S(2)}, u32[]{:S(2)}) collective-permute-start(bf16[128,3584]{1,0:T(8,128)(2,1)} %collective-permute-done.2.refs_2_), channel_id=1, source_target_pairs={{0,448},{64,0},{128,64},{192,128},{256,192},{320,256},{384,320},{4... | collective-permute-start | bytes 2752520 | tf_op jit(solution)/shard_map/ppermute | solution.py:203
  109.6 0.7 copy-start.3
  110.3 32.4 %collective-permute-start.5 = (bf16[128,3584]{1,0:T(8,128)(2,1)S(1)}, bf16[128,3584]{1,0:T(8,128)(2,1)S(1)}, u32[]{:S(2)}, u32[]{:S(2)}) collective-permute-start(bf16[128,3584]{1,0:T(8,128)(2,1)S(1)} %reshape.90.refs_1_), channel_id=1, source_target_pairs={{0,64},{64,128},{128,192},{192,256},{256,320},{320,384},{384,448},... | collective-permute-start | bytes 2752520 | tf_op jit(solution)/shard_map/ppermute | solution.py:203
  112.2 34.2 %collective-permute-start.6 = (bf16[128,3584]{1,0:T(8,128)(2,1)S(1)}, bf16[128,3584]{1,0:T(8,128)(2,1)S(1)}, u32[]{:S(2)}, u32[]{:S(2)}) collective-permute-start(bf16[128,3584]{1,0:T(8,128)(2,1)S(1)} %reshape.90.refs_1_), channel_id=1, source_target_pairs={{0,448},{64,0},{128,64},{192,128},{256,192},{320,256},{384,320},{4... | collective-permute-start | bytes 2752520 | tf_op jit(solution)/shard_map/ppermute | solution.py:203
  146.4 17.6 %copy-start.2 = (bf16[1,1024,448]{1,2,0:T(8,128)(2,1)S(1)}, bf16[1,1024,448]{1,2,0:T(8,128)(2,1)}, u32[]{:S(2)}) copy-start(bf16[1,1024,448]{1,2,0:T(8,128)(2,1)} %param.23) | copy-start | bytes 2752516
  164.0 1.4 copy-start.1
  167.7 19.9 %copy-start.8 = (s32[4]{0:T(128)S(1)}, s32[4]{0:T(128)}, u32[]{:S(2)}) copy-start(s32[4]{0:T(128)} %param.16) | copy-start | bytes 52
  167.7 20.0 %copy-start.9 = (s32[4]{0:T(128)S(1)}, s32[4]{0:T(128)}, u32[]{:S(2)}) copy-start(s32[4]{0:T(128)} %param.15) | copy-start | bytes 52
  167.7 20.1 %copy-start.7 = (bf16[4,2,576]{2,1,0:T(2,128)(2,1)S(1)}, bf16[4,2,576]{2,1,0:T(2,128)(2,1)}, u32[]{:S(2)}) copy-start(bf16[4,2,576]{2,1,0:T(2,128)(2,1)} %param.14) | copy-start | bytes 27652
  169.0 19.2 %copy-start.6 = (bf16[4,256,576]{1,2,0:T(8,128)(2,1)S(1)}, bf16[4,256,576]{1,2,0:T(8,128)(2,1)}, u32[]{:S(2)}) copy-start(bf16[4,256,576]{1,2,0:T(8,128)(2,1)} %param.13) | copy-start | bytes 3538948
  169.0 52.2 %all-to-all-start.3 = ((bf16[512,2,448]{2,1,0:T(2,128)(2,1)}), bf16[512,2,448]{2,1,0:T(2,128)(2,1)S(1)}, u32[]{:S(2)}, u32[]{:S(2)}) async-start(bf16[512,2,448]{2,1,0:T(2,128)(2,1)} %reshape.91), calls=%async_computation.3 | async-start | bytes 2097152 | tf_op jit(solution)/shard_map/all_to_all | solution.py:256
Sparse Core Ops, SparseCore 0:
  110.4 43.1 all-gather.2

commit v3 on v2

--- a/solution.py
+++ b/solution.py
@@ -10,39 +10,53 @@
 LATENT_WIDTH = 512
 
 score_scale = 192.0 ** (-0.5)
+SMEM = pl.BlockSpec(memory_space=pltpu.SMEM)
+HBM = pl.BlockSpec(memory_space=pltpu.HBM)
 VMEM = pl.BlockSpec(memory_space=pltpu.VMEM)
 limit = pltpu.CompilerParams(vmem_limit_bytes=48 * 1024 * 1024)
 
 
-def prepare_kernel(hidden_ref, gain_ref, ids_ref, weights_ref, live_ref, rows_ref, mix_ref):
-    rows, width = hidden_ref.shape
-    x = hidden_ref[...].astype(jnp.float32)
-    meansq = jnp.mean(x * x, -1, keepdims=True)
-    normed = x * lax.rsqrt(meansq + 1e-06) * gain_ref[...]
-    rows_ref[:, :width] = normed.astype(jnp.bfloat16)
-
-    slots = mix_ref.shape[1]
+def prepare_kernel(
+    hidden_hbm, gain_hbm, ids_ref, accepted_ref, rows_ref, out_ref, hidden_ref, gain_ref, sems
+):
+    copies = [
+        pltpu.make_async_copy(hidden_hbm, hidden_ref, sems.at[0]),
+        pltpu.make_async_copy(gain_hbm, gain_ref, sems.at[1]),
+    ]
+    for copy in copies:
+        copy.start()
+    requests, per, width = hidden_ref.shape
+    slots = out_ref.shape[0]
+    rows = requests * per
     lane = lax.broadcasted_iota(jnp.int32, (rows, slots), 1)
-    live = live_ref[...].astype(jnp.float32)
+    row = lax.broadcasted_iota(jnp.int32, (rows, slots), 0)
     named = jnp.zeros((rows, slots), jnp.float32)
-    weight = jnp.zeros((rows, slots), jnp.float32)
-    for p in range(ids_ref.shape[1]):
-        hit = lane // 2 == ids_ref[:, p : p + 1]
-        named += jnp.where(hit, live, 0.0)
-        weight += jnp.where(hit, weights_ref[:, p : p + 1].astype(jnp.float32), 0.0)
-    row = lax.broadcasted_iota(jnp.int32, (rows, slots), 0)
+    for q in range(requests):
+        accepted = jnp.where(accepted_ref[q] != 0, 1.0, 0.0)
+        for t in range(per):
+            hit = jnp.zeros((rows, slots), jnp.bool_)
+            for p in range(ids_ref.shape[2]):
+                hit = hit | (lane // 2 == ids_ref[q, t, p])
+            named += jnp.where(hit & (row == per * q + t), 1.0 if t == 0 else accepted, 0.0)
     rank = jnp.zeros((rows, slots), jnp.float32)
     for r in range(rows - 1):
         rank += jnp.where(row > r, named[r : r + 1, :], 0.0)
     taken = jnp.where(rank == (lane % 2).astype(jnp.float32), named, 0.0)
     rows_ref[:, width:] = taken.astype(jnp.bfloat16)
-    mix_ref[...] = (taken * weight).astype(jnp.bfloat16)
+
+    for copy in copies:
+        copy.wait()
+    x = jnp.concatenate([hidden_ref[q].astype(jnp.float32) for q in range(requests)], axis=0)
+    meansq = jnp.mean(x * x, -1, keepdims=True)
+    normed = x * lax.rsqrt(meansq + 1e-06) * gain_ref[...].reshape(1, width)
+    rows_ref[:, :width] = normed.astype(jnp.bfloat16)
+    dispatch_kernel(rows_ref, out_ref)
 
 
 def dispatch_kernel(rows_ref, out_ref):
     slots, width = out_ref.shape
     taken = rows_ref[:, width:]
-    step = 512
+    step = 256
     for c in range(0, width, step):
         out_ref[:, c : c + step] = lax.dot_general(
             taken,
@@ -50,6 +64,20 @@
             (((0,), (0,)), ((), ())),
             preferred_element_type=jnp.float32,
         ).astype(jnp.bfloat16)
+
+
+def weights_kernel(ids_ref, weights_ref, rows_ref, mix_ref):
+    rows, slots = mix_ref.shape
+    lane = lax.broadcasted_iota(jnp.int32, (rows, slots), 1)
+    row = lax.broadcasted_iota(jnp.int32, (rows, slots), 0)
+    weight = jnp.zeros((rows, slots), jnp.float32)
+    for r in range(rows):
+        q, t = r // ids_ref.shape[1], r % ids_ref.shape[1]
+        for p in range(ids_ref.shape[2]):
+            hit = (row == r) & (lane // 2 == ids_ref[q, t, p])
+            weight += jnp.where(hit, weights_ref[q, t, p], 0.0)
+    taken = rows_ref[:, rows_ref.shape[1] - slots :].astype(jnp.float32)
+    mix_ref[...] = (taken * weight).astype(jnp.bfloat16)
 
 
 def inner_piece(rows, weight):
@@ -71,7 +99,7 @@
         at += 1
 
 
-def last_inner_kernel(weight_ref, *refs):
+def late_inner_kernel(weight_ref, *refs):
     out_ref = refs[-1]
     for i, rows_ref in enumerate(refs[:-1]):
         piece = inner_piece(rows_ref[...], weight_ref[...])
@@ -79,14 +107,14 @@
             out_ref[r, i] = piece
 
 
-def down_kernel(first_places, last_places, first_ref, last_ref, weight_ref, out_ref):
-    count, slots = first_ref.shape[0], first_ref.shape[2]
+def down_kernel(places, *refs):
+    *inner_refs, weight_ref, out_ref = refs
+    count, slots = inner_refs[0].shape[0], inner_refs[0].shape[2]
 
     def piece(r, home):
-        place = (home - r) % count
-        if place in first_places:
-            return first_ref[r, first_places.index(place)]
-        return last_ref[r, last_places.index(place)]
+        for ref, here in zip(inner_refs, places):
+            if (home - r) % count in here:
+                return ref[r, here.index((home - r) % count)]
 
     for home in range(count):
         full = jnp.concatenate([piece(r, home) for r in range(count)], axis=1)
@@ -97,13 +125,16 @@
 
 def mix_kernel(mix_ref, back_ref, out_ref):
     mix = mix_ref[...]
-    out_ref[...] = jnp.concatenate(
+    routed = jnp.concatenate(
         [
             jnp.dot(mix, back_ref[c], preferred_element_type=jnp.float32)
             for c in range(back_ref.shape[0])
         ],
         axis=1,
-    ).astype(jnp.bfloat16)
+    )
+    requests, per, _ = out_ref.shape
+    for q in range(requests):
+        out_ref[q] = routed[per * q : per * (q + 1), :].astype(jnp.bfloat16)
 
 
 def attend(queries, latent_key_cache, fresh_latent_keys, lengths, row_live):
@@ -157,7 +188,6 @@
 ):
     nreq = queries.shape[0]
     width = hidden.shape[2]
-    picks = expert_ids.shape[2]
     nrep = lax.axis_size("rep")
     experts = lax.axis_size("ep")
     rows = nreq * 2
@@ -166,38 +196,36 @@
     slots = 2 * experts
     row_live = jnp.stack([jnp.ones_like(accepted), accepted], 1)
 
-    tagged, mix = pl.pallas_call(
+    tagged, buffer = pl.pallas_call(
         prepare_kernel,
         out_shape=(
             jax.ShapeDtypeStruct((rows, width + slots), jnp.bfloat16),
-            jax.ShapeDtypeStruct((rows, slots), jnp.bfloat16),
+            jax.ShapeDtypeStruct((slots, width), jnp.bfloat16),
         ),
-        in_specs=[VMEM] * 5,
-        out_specs=(VMEM, VMEM),
+        in_specs=[HBM, HBM, SMEM, SMEM],
+        out_specs=(VMEM,) * 2,
+        scratch_shapes=[
+            pltpu.VMEM(hidden.shape, hidden.dtype),
+            pltpu.VMEM(norm_gain.shape, norm_gain.dtype),
+            pltpu.SemaphoreType.DMA((2,)),
+        ],
         compiler_params=limit,
         name="prepare",
-    )(
-        hidden.reshape(rows, width),
-        norm_gain.reshape(1, width),
-        expert_ids.reshape(rows, picks),
-        router_weights.reshape(rows, picks),
-        row_live.reshape(rows, 1),
-    )
-
-    def dispatch(rows_in):
-        return pl.pallas_call(
-            dispatch_kernel,
-            out_shape=jax.ShapeDtypeStruct((slots, width), jnp.bfloat16),
-            in_specs=[VMEM],
-            out_specs=VMEM,
-            compiler_params=limit,
-            name="dispatch",
-        )(rows_in).reshape(experts, 2, width)
+    )(hidden, norm_gain, expert_ids, accepted)
+    mix = pl.pallas_call(
+        weights_kernel,
+        out_shape=jax.ShapeDtypeStruct((rows, slots), jnp.bfloat16),
+        in_specs=[SMEM, SMEM, VMEM],
+        out_specs=VMEM,
+        compiler_params=limit,
+        name="weights",
+    )(expert_ids, router_weights.astype(jnp.float32), tagged)
 
     def to_experts(buffer):
-        return lax.all_to_all(buffer, "ep", split_axis=0, concat_axis=0, tiled=True).reshape(
-            slots, width
-        )
+        columns = buffer.shape[1]
+        return lax.all_to_all(
+            buffer.reshape(experts, 2, columns), "ep", split_axis=0, concat_axis=0, tiled=True
+        ).reshape(slots, columns)
 
     def shift(x, by):
         return lax.ppermute(x, "rep", [(i, (i + by) % nrep) for i in range(nrep)])
@@ -213,44 +241,53 @@
             in_specs=[VMEM] * (1 + len(before) + n),
             out_specs=VMEM,
             compiler_params=limit,
-            cost_estimate=pl.CostEstimate(
-                flops=4 * n * slots * width * units,
-                bytes_accessed=2 * width * (2 * units + n * slots),
-                transcendentals=n * slots * units,
-            ),
             name="inner",
         )(both_weight, *before, *blocks)
 
+    def dispatch(rows_in):
+        return pl.pallas_call(
+            dispatch_kernel,
+            out_shape=jax.ShapeDtypeStruct((slots, width), jnp.bfloat16),
+            in_specs=[VMEM],
+            out_specs=VMEM,
+            compiler_params=limit,
+            name="dispatch",
+        )(rows_in)
+
     half = nrep // 2
     far_rows = shift(tagged, half)
-    own = to_experts(dispatch(tagged))
+    own = to_experts(buffer)
     own, far_buffer = lax.optimization_barrier((own, dispatch(far_rows)))
+    up_one, down_one = shift(own, 1), shift(own, -1)
+    at_home, far_buffer = lax.optimization_barrier((inner_blocks([], own), far_buffer))
     far = to_experts(far_buffer)
-    up_one, down_one = shift(own, 1), shift(own, -1)
-    near = inner_blocks([], own, up_one, down_one)
+    near = inner_blocks([at_home], up_one, down_one)
     up_two, down_two = shift(up_one, 1), shift(down_one, -1)
     up_far, down_far = shift(far, 1), shift(far, -1)
-    first_places = [0, nrep - 1, 1, half, nrep - 2, 2]
-    first = inner_blocks([near], far, up_two, down_two)
-    first = lax.all_gather(first, "rep", axis=0, tiled=False)
-    last_places = [half - 1, half + 1]
-    last = pl.pallas_call(
-        last_inner_kernel,
-        out_shape=jax.ShapeDtypeStruct((nrep, 2, slots, units), jnp.bfloat16),
-        in_specs=[VMEM] * 3,
-        out_specs=VMEM,
-        compiler_params=limit,
-        name="last_inner",
-    )(both_weight, up_far, down_far)
-    last = lax.all_to_all(last, "rep", split_axis=0, concat_axis=0, tiled=True)
+    first_places = [0, nrep - 1, 1, half]
+    first = lax.all_gather(inner_blocks([near], far), "rep", axis=0, tiled=False)
+
+    def late_blocks(*blocks):
+        pieces = pl.pallas_call(
+            late_inner_kernel,
+            out_shape=jax.ShapeDtypeStruct((nrep, len(blocks), slots, units), jnp.bfloat16),
+            in_specs=[VMEM] * (1 + len(blocks)),
+            out_specs=VMEM,
+            compiler_params=limit,
+            name="late_inner",
+        )(both_weight, *blocks)
+        return lax.all_to_all(pieces, "rep", split_axis=0, concat_axis=0, tiled=True)
+
+    second, third = late_blocks(up_two, down_two), late_blocks(up_far, down_far)
+    places = [first_places, [nrep - 2, 2], [half - 1, half + 1]]
     expert_out = pl.pallas_call(
-        partial(down_kernel, first_places, last_places),
+        partial(down_kernel, places),
         out_shape=jax.ShapeDtypeStruct((nrep * slots, part), jnp.bfloat16),
-        in_specs=[VMEM] * 3,
+        in_specs=[VMEM] * 4,
         out_specs=VMEM,
         compiler_params=limit,
         name="down",
-    )(first, last, jnp.swapaxes(down_weight[0], 0, 1))
+    )(first, second, third, jnp.swapaxes(down_weight[0], 0, 1))
     queries, expert_out = lax.optimization_barrier((queries, expert_out))
     attended = attend(queries, latent_key_cache, fresh_latent_keys, lengths, row_live)
     back = lax.all_to_all(
@@ -262,13 +299,13 @@
     ).reshape(nrep, slots, part)
     routed = pl.pallas_call(
         mix_kernel,
-        out_shape=jax.ShapeDtypeStruct((rows, width), jnp.bfloat16),
+        out_shape=jax.ShapeDtypeStruct((nreq, 2, width), jnp.bfloat16),
         in_specs=[VMEM] * 2,
         out_specs=VMEM,
         compiler_params=limit,
         name="mix",
     )(mix, back)
-    return attended, routed.reshape(nreq, 2, width)
+    return attended, routed
 
 
 def solution(mesh):

time: 231 us -> 230 us (level)
  blocking collectives: 16.9 us -> 0 us
  starting transfers between devices: 73.9 us -> 82.4 us
  Pallas kernels: 8.91 us -> 16.6 us
    all_to_all x2 -> x4, waiting for transfers between devices: 14.8 us -> 43.4 us  [the longest x2 22.2 us: to_experts(): lax.all_to_all(buffer.reshape(experts, 2, columns), 'ep', split_axis=0, c...]
    ppermute x7, waiting for transfers between devices: 51.8 us -> 24.3 us  [shift(): return lax.ppermute(x, 'rep', [(i, (i + by) % nrep) for i in range(nrep)])]
    all_to_all x1 -> x0, blocking collectives: 16.9 us -> none  [per_device(): last = lax.all_to_all(last, 'rep', split_axis=0, concat_axis=0, tiled=True)]
    all_to_all x2 -> x4, starting transfers between devices: 18.3 us -> 32.9 us  [the longest x2 18.3 us: to_experts(): lax.all_to_all(buffer.reshape(experts, 2, columns), 'ep', split_axis=0, c...]
    pallas_call x3 -> x5, Pallas kernels: 3.24 us -> 10.2 us  [the longest x2 5.16 us: late_blocks(): pl.pallas_call(late_inner_kernel, out_shape=jax.ShapeDtypeStruct((nrep, l...]
    all_to_all x1, starting transfers between devices: 18.6 us -> 13.2 us  [per_device(): lax.all_to_all(expert_out.reshape(nrep * experts, 2, part), ('rep', 'ep')...]
    reshape x8 -> x4, local copies, waits for them, and re-layouts: 7.68 us -> 6.33 us  [the longest x2 3.75 us: to_experts(): return lax.all_to_all(buffer.reshape(experts, 2, columns), 'ep', split_ax...]
    unnamed x21 -> x32, local copies, waits for them, and re-layouts: 4.29 us -> 5.01 us
  transfers between devices with their start and end apart: 11 -> 13, of which waited for: 9 -> 9; matrix products, arithmetic and copies ran while one was open for 4% -> 4% of each run, Pallas kernels for 2% -> 5%
where the time goes in v3:
time: 230 us; the launch traced here: 229 us
  waiting for transfers between devices  96.2 us (42%)
  starting transfers between devices  82.4 us (36%)
  Pallas kernels  16.6 us (7%)
  between operations  14.4 us (6%)
  local copies, waits for them, and re-layouts  13.6 us (6%)
  matrix products  3.84 us (2%)
    ppermute x7, starting transfers between devices, shift(): return lax.ppermute(x, 'rep', [(i, (i + by) % nrep) for i in range(nrep)])  36.2 us
    all_to_all x1, waiting for transfers between devices, per_device(): lax.all_to_all(expert_out.reshape(nrep * experts, 2, part), ('rep', 'ep')...  28.4 us
    ppermute x7, waiting for transfers between devices, shift(): return lax.ppermute(x, 'rep', [(i, (i + by) % nrep) for i in range(nrep)])  24.3 us
    all_to_all x2, waiting for transfers between devices, to_experts(): lax.all_to_all(buffer.reshape(experts, 2, columns), 'ep', split_axis=0, c...  22.2 us
    all_to_all x2, waiting for transfers between devices, late_blocks(): lax.all_to_all(pieces, 'rep', split_axis=0, concat_axis=0, tiled=True)  21.2 us
    all_to_all x2, starting transfers between devices, to_experts(): lax.all_to_all(buffer.reshape(experts, 2, columns), 'ep', split_axis=0, c...  18.3 us
    all_to_all x2, starting transfers between devices, late_blocks(): lax.all_to_all(pieces, 'rep', split_axis=0, concat_axis=0, tiled=True)  14.6 us
    all_to_all x1, starting transfers between devices, per_device(): lax.all_to_all(expert_out.reshape(nrep * experts, 2, part), ('rep', 'ep')...  13.2 us
  transfers between devices with their start and end apart: 13, of which 9 were waited for; matrix products, arithmetic and copies ran while one was open for 4% of the time, Pallas kernels for 5%

profile of v3, /device:TPU:1, one launch (start us, length us, event | category | flops | bytes accessed | tf_op | source)
XLA Modules:
  0.0 229.0 jit_solution(18079160438034058031)
XLA Ops:
  11.4 1.3 reshape.64
  12.7 11.6 %all-to-all-start = ((bf16[64,2,3584]{2,1,0:T(2,128)(2,1)}), bf16[64,2,3584]{2,1,0:T(2,128)(2,1)S(1)}, u32[]{:S(2)}, u32[]{:S(2)}) async-start(bf16[64,2,3584]{2,1,0:T(2,128)(2,1)} %reshape.64), calls=%async_computation | async-start | bytes 1835008 | tf_op jit(solution)/shard_map/all_to_all | solution.py:226
  24.3 10.6 %collective-permute-start = (bf16[8,3712]{1,0:T(8,128)(2,1)S(1)}, bf16[8,3712]{1,0:T(8,128)(2,1)S(1)}, u32[]{:S(2)}, u32[]{:S(2)}) collective-permute-start(bf16[8,3712]{1,0:T(8,128)(2,1)S(1)} %get-tuple-element.11.rows_ref), channel_id=1, source_target_pairs={{0,256},{64,320},{128,384},{192,448},{256,0},{320,64},{384,128},{4... | collective-permute-start | bytes 178184 | tf_op jit(solution)/shard_map/ppermute | solution.py:231
  35.0 1.9 collective-permute-done.rows_ref
  37.3 12.8 %all-to-all-done = bf16[64,2,3584]{2,1,0:T(2,128)(2,1)S(1)} async-done(((bf16[64,2,3584]{2,1,0:T(2,128)(2,1)}), bf16[64,2,3584]{2,1,0:T(2,128)(2,1)S(1)}, u32[]{:S(2)}, u32[]{:S(2)}) %all-to-all-start) | async-done | bytes 917536 | tf_op jit(solution)/shard_map/all_to_all | solution.py:226
  51.3 4.0 %collective-permute-start.1 = (bf16[128,3584]{1,0:T(8,128)(2,1)}, bf16[128,3584]{1,0:T(8,128)(2,1)}, u32[]{:S(2)}, u32[]{:S(2)}) collective-permute-start(bf16[128,3584]{1,0:T(8,128)(2,1)} %reshape.65.refs_0_), channel_id=1, source_target_pairs={{0,64},{64,128},{128,192},{192,256},{256,320},{320,384},{384,448},... | collective-permute-start | bytes 2752520 | tf_op jit(solution)/shard_map/ppermute | solution.py:231
  55.3 8.6 %collective-permute-start.2 = (bf16[128,3584]{1,0:T(8,128)(2,1)}, bf16[128,3584]{1,0:T(8,128)(2,1)}, u32[]{:S(2)}, u32[]{:S(2)}) collective-permute-start(bf16[128,3584]{1,0:T(8,128)(2,1)} %reshape.65.refs_0_), channel_id=1, source_target_pairs={{0,448},{64,0},{128,64},{192,128},{256,192},{320,256},{384,320},{4... | collective-permute-start | bytes 2752520 | tf_op jit(solution)/shard_map/ppermute | solution.py:231
  63.9 1.7 pad_maximum_fusion.weight_ref
  65.6 1.6 inner.3.refs_0_
  67.2 1.3 reshape.66
  68.5 6.7 %all-to-all-start.1 = ((bf16[64,2,3584]{2,1,0:T(2,128)(2,1)}), bf16[64,2,3584]{2,1,0:T(2,128)(2,1)}, u32[]{:S(2)}, u32[]{:S(2)}) async-start(bf16[64,2,3584]{2,1,0:T(2,128)(2,1)} %reshape.66), calls=%async_computation.1 | async-start | bytes 1835008 | tf_op jit(solution)/shard_map/all_to_all | solution.py:226
  75.2 7.5 %collective-permute-done.1.refs_1_ = bf16[128,3584]{1,0:T(8,128)(2,1)} collective-permute-done((bf16[128,3584]{1,0:T(8,128)(2,1)}, bf16[128,3584]{1,0:T(8,128)(2,1)}, u32[]{:S(2)}, u32[]{:S(2)}) %collective-permute-start.1) | collective-permute-done | bytes 917536 | tf_op jit(solution)/shard_map/ppermute | solution.py:231
  82.8 1.9 collective-permute-start.3
  84.7 4.6 %collective-permute-start.4 = (bf16[128,3584]{1,0:T(8,128)(2,1)}, bf16[128,3584]{1,0:T(8,128)(2,1)}, u32[]{:S(2)}, u32[]{:S(2)}) collective-permute-start(bf16[128,3584]{1,0:T(8,128)(2,1)} %collective-permute-done.2.refs_2_), channel_id=1, source_target_pairs={{0,448},{64,0},{128,64},{192,128},{256,192},{320,256},{384,320},{4... | collective-permute-start | bytes 2752520 | tf_op jit(solution)/shard_map/ppermute | solution.py:231
  89.3 2.1 inner.4.refs_0_
  91.4 9.4 %all-to-all-done.1 = bf16[64,2,3584]{2,1,0:T(2,128)(2,1)} async-done(((bf16[64,2,3584]{2,1,0:T(2,128)(2,1)}), bf16[64,2,3584]{2,1,0:T(2,128)(2,1)}, u32[]{:S(2)}, u32[]{:S(2)}) %all-to-all-start.1) | async-done | bytes 917536 | tf_op jit(solution)/shard_map/all_to_all | solution.py:226
  100.9 2.5 %reshape.67.refs_1_ = bf16[128,3584]{1,0:T(8,128)(2,1)S(1)} reshape(bf16[64,2,3584]{2,1,0:T(2,128)(2,1)} %all-to-all-done.1) | data formatting | bytes 1835008 | tf_op jit(solution)/shard_map/reshape | solution.py:228
  103.3 1.9 collective-permute-start.5
  105.3 4.6 %collective-permute-start.6 = (bf16[128,3584]{1,0:T(8,128)(2,1)S(1)}, bf16[128,3584]{1,0:T(8,128)(2,1)}, u32[]{:S(2)}, u32[]{:S(2)}) collective-permute-start(bf16[128,3584]{1,0:T(8,128)(2,1)S(1)} %reshape.67.refs_1_), channel_id=1, source_target_pairs={{0,448},{64,0},{128,64},{192,128},{256,192},{320,256},{384,320},{4... | collective-permute-start | bytes 2752520 | tf_op jit(solution)/shard_map/ppermute | solution.py:231
  111.0 2.1 late_inner.2
  113.9 4.2 %all-to-all-start.2 = ((bf16[8,2,128,128]{3,2,1,0:T(8,128)(2,1)}), bf16[8,2,128,128]{3,2,1,0:T(8,128)(2,1)}, u32[]{:S(2)}, u32[]{:S(2)}) async-start(bf16[8,2,128,128]{3,2,1,0:T(8,128)(2,1)} %copy-done.1), calls=%async_computation.2 | async-start | bytes 1048576 | tf_op jit(solution)/shard_map/all_to_all | solution.py:279
  118.1 12.9 %collective-permute-done.5.refs_0_ = bf16[128,3584]{1,0:T(8,128)(2,1)} collective-permute-done((bf16[128,3584]{1,0:T(8,128)(2,1)S(1)}, bf16[128,3584]{1,0:T(8,128)(2,1)}, u32[]{:S(2)}, u32[]{:S(2)}) %collective-permute-start.5) | collective-permute-done | bytes 917536 | tf_op jit(solution)/shard_map/ppermute | solution.py:231
  131.0 2.0 collective-permute-done.6.refs_1_
  133.0 3.0 %late_inner.3 = bf16[8,2,128,128]{3,2,1,0:T(8,128)(2,1)} custom-call(bf16[3584,256]{1,0:T(8,128)(2,1)S(1)} %pad_maximum_fusion.weight_ref, bf16[128,3584]{1,0:T(8,128)(2,1)} %collective-permute-done.5.refs_0_, bf16[128,3584]{1,0:T(8,128)(2,1)} %collective-permute-done.6.refs_1_), custom_call_target="tpu_custom_call" | custom-call | tf_op jit(solution)/shard_map/late_inner/pallas_call | solution.py:271
  136.0 7.3 %all-to-all-done.2.refs_1_ = bf16[8,2,128,128]{3,2,1,0:T(8,128)(2,1)} async-done(((bf16[8,2,128,128]{3,2,1,0:T(8,128)(2,1)}), bf16[8,2,128,128]{3,2,1,0:T(8,128)(2,1)}, u32[]{:S(2)}, u32[]{:S(2)}) %all-to-all-start.2) | async-done | bytes 524320 | tf_op jit(solution)/shard_map/all_to_all | solution.py:279
  143.3 10.4 %all-to-all-start.3 = ((bf16[8,2,128,128]{3,2,1,0:T(8,128)(2,1)}), bf16[8,2,128,128]{3,2,1,0:T(8,128)(2,1)S(1)}, u32[]{:S(2)}, u32[]{:S(2)}) async-start(bf16[8,2,128,128]{3,2,1,0:T(8,128)(2,1)} %late_inner.3), calls=%async_computation.3 | async-start | bytes 1048576 | tf_op jit(solution)/shard_map/all_to_all | solution.py:279
  153.7 13.9 %all-to-all-done.3.refs_2_ = bf16[8,2,128,128]{3,2,1,0:T(8,128)(2,1)S(1)} async-done(((bf16[8,2,128,128]{3,2,1,0:T(8,128)(2,1)}), bf16[8,2,128,128]{3,2,1,0:T(8,128)(2,1)S(1)}, u32[]{:S(2)}, u32[]{:S(2)}) %all-to-all-start.3) | async-done | bytes 524320 | tf_op jit(solution)/shard_map/all_to_all | solution.py:279
  168.8 3.3 %down.1 = bf16[1024,448]{1,0:T(8,128)(2,1)S(1)} custom-call(bf16[8,4,128,128]{3,2,1,0:T(8,128)(2,1)S(1)} %bitcast.34, bf16[8,2,128,128]{3,2,1,0:T(8,128)(2,1)} %all-to-all-done.2.refs_1_, bf16[8,2,128,128]{3,2,1,0:T(8,128)(2,1)S(1)} %all-to-all-done.3.refs_2_, bf16[448,1024]{1,0:T(8,128)(2,1)S(1)} %bitcast.35), custom_call_target="tpu_custom_call" | custom-call | tf_op jit(solution)/shard_map/down/pallas_call | solution.py:283
  172.2 1.3 reshape.68
  173.5 13.2 %all-to-all-start.4 = ((bf16[512,2,448]{2,1,0:T(2,128)(2,1)}), bf16[512,2,448]{2,1,0:T(2,128)(2,1)S(1)}, u32[]{:S(2)}, u32[]{:S(2)}) async-start(bf16[512,2,448]{2,1,0:T(2,128)(2,1)} %reshape.68), calls=%async_computation.4 | async-start | bytes 2097152 | tf_op jit(solution)/shard_map/all_to_all | solution.py:293
  188.2 1.7 fusion.17
  191.9 28.4 %all-to-all-done.4 = bf16[512,2,448]{2,1,0:T(2,128)(2,1)S(1)} async-done(((bf16[512,2,448]{2,1,0:T(2,128)(2,1)}), bf16[512,2,448]{2,1,0:T(2,128)(2,1)S(1)}, u32[]{:S(2)}, u32[]{:S(2)}) %all-to-all-start.4) | async-done | bytes 917536 | tf_op jit(solution)/shard_map/all_to_all | solution.py:293
  (57 shorter events, 14.2 us)
Async XLA Ops:
  7.2 180.6 %copy-start = (bf16[4,2,64,576]{3,2,1,0:T(8,128)(2,1)S(1)}, bf16[4,2,64,576]{3,2,1,0:T(8,128)(2,1)}, u32[]{:S(2)}) copy-start(bf16[4,2,64,576]{3,2,1,0:T(8,128)(2,1)} %param.12) | copy-start | bytes 1769476
  7.2 0.9 copy-start.6
  8.1 0.7 copy-start.7
  8.8 0.7 copy-start.8
  9.5 0.7 copy-start.10
  11.4 12.9 %copy-start.4 = (bf16[8,3712]{1,0:T(8,128)(2,1)}, bf16[8,3712]{1,0:T(8,128)(2,1)S(1)}, u32[]{:S(2)}) copy-start(bf16[8,3712]{1,0:T(8,128)(2,1)S(1)} %get-tuple-element.11.rows_ref) | copy-start | bytes 178180
  12.7 37.4 %all-to-all-start = ((bf16[64,2,3584]{2,1,0:T(2,128)(2,1)}), bf16[64,2,3584]{2,1,0:T(2,128)(2,1)S(1)}, u32[]{:S(2)}, u32[]{:S(2)}) async-start(bf16[64,2,3584]{2,1,0:T(2,128)(2,1)} %reshape.64), calls=%async_computation | async-start | bytes 1835008 | tf_op jit(solution)/shard_map/all_to_all | solution.py:226
  24.3 12.5 %collective-permute-start = (bf16[8,3712]{1,0:T(8,128)(2,1)S(1)}, bf16[8,3712]{1,0:T(8,128)(2,1)S(1)}, u32[]{:S(2)}, u32[]{:S(2)}) collective-permute-start(bf16[8,3712]{1,0:T(8,128)(2,1)S(1)} %get-tuple-element.11.rows_ref), channel_id=1, source_target_pairs={{0,256},{64,320},{128,384},{192,448},{256,0},{320,64},{384,128},{4... | collective-permute-start | bytes 178184 | tf_op jit(solution)/shard_map/ppermute | solution.py:231
  51.3 31.4 %collective-permute-start.1 = (bf16[128,3584]{1,0:T(8,128)(2,1)}, bf16[128,3584]{1,0:T(8,128)(2,1)}, u32[]{:S(2)}, u32[]{:S(2)}) collective-permute-start(bf16[128,3584]{1,0:T(8,128)(2,1)} %reshape.65.refs_0_), channel_id=1, source_target_pairs={{0,64},{64,128},{128,192},{192,256},{256,320},{320,384},{384,448},... | collective-permute-start | bytes 2752520 | tf_op jit(solution)/shard_map/ppermute | solution.py:231
  55.3 29.3 %collective-permute-start.2 = (bf16[128,3584]{1,0:T(8,128)(2,1)}, bf16[128,3584]{1,0:T(8,128)(2,1)}, u32[]{:S(2)}, u32[]{:S(2)}) collective-permute-start(bf16[128,3584]{1,0:T(8,128)(2,1)} %reshape.65.refs_0_), channel_id=1, source_target_pairs={{0,448},{64,0},{128,64},{192,128},{256,192},{320,256},{384,320},{4... | collective-permute-start | bytes 2752520 | tf_op jit(solution)/shard_map/ppermute | solution.py:231
  68.5 32.4 %all-to-all-start.1 = ((bf16[64,2,3584]{2,1,0:T(2,128)(2,1)}), bf16[64,2,3584]{2,1,0:T(2,128)(2,1)}, u32[]{:S(2)}, u32[]{:S(2)}) async-start(bf16[64,2,3584]{2,1,0:T(2,128)(2,1)} %reshape.66), calls=%async_computation.1 | async-start | bytes 1835008 | tf_op jit(solution)/shard_map/all_to_all | solution.py:226
  75.2 78.5 %all-gather.3.cloned.1.call-start = ((), (), s32[]{:S(2)}) async-start(), calls=%async_computation.5 | async-start | bytes 1179648 | tf_op jit(solution)/shard_map/all_gather | solution.py:268
  82.8 28.2 %collective-permute-start.3 = (bf16[128,3584]{1,0:T(8,128)(2,1)}, bf16[128,3584]{1,0:T(8,128)(2,1)}, u32[]{:S(2)}, u32[]{:S(2)}) collective-permute-start(bf16[128,3584]{1,0:T(8,128)(2,1)} %collective-permute-done.1.refs_1_), channel_id=1, source_target_pairs={{0,64},{64,128},{128,192},{192,256},{256,320},{320,384},{384,448},... | collective-permute-start | bytes 2752520 | tf_op jit(solution)/shard_map/ppermute | solution.py:231
  84.7 26.3 %collective-permute-start.4 = (bf16[128,3584]{1,0:T(8,128)(2,1)}, bf16[128,3584]{1,0:T(8,128)(2,1)}, u32[]{:S(2)}, u32[]{:S(2)}) collective-permute-start(bf16[128,3584]{1,0:T(8,128)(2,1)} %collective-permute-done.2.refs_2_), channel_id=1, source_target_pairs={{0,448},{64,0},{128,64},{192,128},{256,192},{320,256},{384,320},{4... | collective-permute-start | bytes 2752520 | tf_op jit(solution)/shard_map/ppermute | solution.py:231
  103.3 27.6 %collective-permute-start.5 = (bf16[128,3584]{1,0:T(8,128)(2,1)S(1)}, bf16[128,3584]{1,0:T(8,128)(2,1)}, u32[]{:S(2)}, u32[]{:S(2)}) collective-permute-start(bf16[128,3584]{1,0:T(8,128)(2,1)S(1)} %reshape.67.refs_1_), channel_id=1, source_target_pairs={{0,64},{64,128},{128,192},{192,256},{256,320},{320,384},{384,448},... | collective-permute-start | bytes 2752520 | tf_op jit(solution)/shard_map/ppermute | solution.py:231
  105.3 27.7 %collective-permute-start.6 = (bf16[128,3584]{1,0:T(8,128)(2,1)S(1)}, bf16[128,3584]{1,0:T(8,128)(2,1)}, u32[]{:S(2)}, u32[]{:S(2)}) collective-permute-start(bf16[128,3584]{1,0:T(8,128)(2,1)S(1)} %reshape.67.refs_1_), channel_id=1, source_target_pairs={{0,448},{64,0},{128,64},{192,128},{256,192},{320,256},{384,320},{4... | collective-permute-start | bytes 2752520 | tf_op jit(solution)/shard_map/ppermute | solution.py:231
  113.1 0.8 copy-start.1
  113.9 29.4 %all-to-all-start.2 = ((bf16[8,2,128,128]{3,2,1,0:T(8,128)(2,1)}), bf16[8,2,128,128]{3,2,1,0:T(8,128)(2,1)}, u32[]{:S(2)}, u32[]{:S(2)}) async-start(bf16[8,2,128,128]{3,2,1,0:T(8,128)(2,1)} %copy-done.1), calls=%async_computation.2 | async-start | bytes 1048576 | tf_op jit(solution)/shard_map/all_to_all | solution.py:279
  133.0 34.6 %copy-start.3 = (bf16[1,1024,448]{1,2,0:T(8,128)(2,1)S(1)}, bf16[1,1024,448]{1,2,0:T(8,128)(2,1)}, u32[]{:S(2)}) copy-start(bf16[1,1024,448]{1,2,0:T(8,128)(2,1)} %param.23) | copy-start | bytes 2752516
  143.3 24.3 %all-to-all-start.3 = ((bf16[8,2,128,128]{3,2,1,0:T(8,128)(2,1)}), bf16[8,2,128,128]{3,2,1,0:T(8,128)(2,1)S(1)}, u32[]{:S(2)}, u32[]{:S(2)}) async-start(bf16[8,2,128,128]{3,2,1,0:T(8,128)(2,1)} %late_inner.3), calls=%async_computation.3 | async-start | bytes 1048576 | tf_op jit(solution)/shard_map/all_to_all | solution.py:279
  167.6 1.2 copy-start.2
  172.1 14.6 %copy-start.11 = (s32[4]{0:T(128)S(1)}, s32[4]{0:T(128)}, u32[]{:S(2)}) copy-start(s32[4]{0:T(128)} %accepted_ref.1) | copy-start | bytes 52
  172.1 14.7 %copy-start.14 = (bf16[4,2,8]{2,1,0:T(2,128)(2,1)S(1)}, bf16[4,2,8]{2,1,0:T(2,128)(2,1)}, u32[]{:S(2)}) copy-start(bf16[4,2,8]{2,1,0:T(2,128)(2,1)} %param.20) | copy-start | bytes 388
  172.1 14.7 %copy-start.5 = (bf16[8,3712]{1,0:T(8,128)(2,1)S(1)}, bf16[8,3712]{1,0:T(8,128)(2,1)}, u32[]{:S(2)}) copy-start(bf16[8,3712]{1,0:T(8,128)(2,1)} %copy-done.4) | copy-start | bytes 178180
  172.2 14.7 %copy-start.9 = (s32[4,2,8]{2,1,0:T(2,128)S(1)}, s32[4,2,8]{2,1,0:T(2,128)}, u32[]{:S(2)}) copy-start(s32[4,2,8]{2,1,0:T(2,128)} %ids_ref.3) | copy-start | bytes 772
  172.2 15.5 %copy-start.15 = (s32[4]{0:T(128)S(1)}, s32[4]{0:T(128)}, u32[]{:S(2)}) copy-start(s32[4]{0:T(128)} %param.15) | copy-start | bytes 52
  172.2 15.5 %copy-start.13 = (bf16[4,2,576]{2,1,0:T(2,128)(2,1)S(1)}, bf16[4,2,576]{2,1,0:T(2,128)(2,1)}, u32[]{:S(2)}) copy-start(bf16[4,2,576]{2,1,0:T(2,128)(2,1)} %param.14) | copy-start | bytes 27652
  173.5 46.9 %all-to-all-start.4 = ((bf16[512,2,448]{2,1,0:T(2,128)(2,1)}), bf16[512,2,448]{2,1,0:T(2,128)(2,1)S(1)}, u32[]{:S(2)}, u32[]{:S(2)}) async-start(bf16[512,2,448]{2,1,0:T(2,128)(2,1)} %reshape.68), calls=%async_computation.4 | async-start | bytes 2097152 | tf_op jit(solution)/shard_map/all_to_all | solution.py:293
  187.6 2.6 %copy-start.12 = (bf16[4,256,576]{1,2,0:T(8,128)(2,1)S(1)}, bf16[4,256,576]{1,2,0:T(8,128)(2,1)}, u32[]{:S(2)}) copy-start(bf16[4,256,576]{1,2,0:T(8,128)(2,1)} %param.13) | copy-start | bytes 3538948
Sparse Core Ops, SparseCore 0:
  111.1 42.0 all-gather.2
